TPU v7x, 32 devices: a whole 2x2x4 slice. The times are simulated.
32 devices in a mesh: rep: 2 (over core), fsdp: 16 (over z, y, x).
Axes of the slice: x: 2, y: 2, z: 4, core: 2. Of those that a mesh axis runs over, the one named last changes fastest.
Arguments:
- inputs: bfloat16 [32, 1024, 768], P(('rep', 'fsdp')), may hold values from -6 to 6
- cotangent: bfloat16 [32, 1024, 768], P(('rep', 'fsdp')), may hold values from -6 to 6
- seg_sizes: int32 [32, 8], P(('rep', 'fsdp')), may hold values from 0 to 1024, as said below
- seq_lengths: int32 [32, 8], P(('rep', 'fsdp')), may hold values from 0 to 1024, as said below
- timesteps: int32 [32, 8], P(('rep', 'fsdp')), may hold values from 0 to 999
- absorbed: int32 [32, 1024], P(('rep', 'fsdp')), may hold values 0 or 1
- qkv_weight: float32 [768, 2304], P('fsdp'), may hold values from -0.2 to 0.2
- out_weight: float32 [768, 768], P('fsdp'), may hold values from -2.5 to 2.5
- up_weight: float32 [768, 3072], P('fsdp'), may hold values from -0.25 to 0.25
- down_weight: float32 [3072, 768], P('fsdp'), may hold values from -0.7 to 0.7
- mod_weight: float32 [128, 4608], P(None, 'fsdp'), may hold values from -4 to 4
- qkv_first: float32 [768, 2304], P('fsdp'), may hold values from -27.1529 to 27.1529
- out_first: float32 [768, 768], P('fsdp'), may hold values from -2.2627417 to 2.2627417
- up_first: float32 [768, 3072], P('fsdp'), may hold values from -108.6116 to 108.6116
- down_first: float32 [3072, 768], P('fsdp'), may hold values from -43.44464 to 43.44464
- mod_first: float32 [128, 4608], P(None, 'fsdp'), may hold values from -23.532514 to 23.532514
- qkv_second: float32 [768, 2304], P('fsdp'), may hold values from 0 to 18.56
- out_second: float32 [768, 768], P('fsdp'), may hold values from 0 to 0.1312
- up_second: float32 [768, 3072], P('fsdp'), may hold values from 0 to 298.1888
- down_second: float32 [3072, 768], P('fsdp'), may hold values from 0 to 49.152
- mod_second: float32 [128, 4608], P(None, 'fsdp'), may hold values from 0 to 13.1072
- vectors: float32 [9984], P('fsdp'), may hold values from -1.2 to 3.8
- vectors_first: float32 [9984], P('fsdp'), may hold values from -38.01406 to 38.01406
- vectors_second: float32 [9984], P('fsdp'), may hold values from 0 to 36.0448
Outputs:
- out_hidden: bfloat16 [32, 1024, 768], P(('rep', 'fsdp'))
- grad_inputs: float32 [32, 1024, 768], P(('rep', 'fsdp'))
- qkv_updated: float32 [768, 2304], P('fsdp')
- out_updated: float32 [768, 768], P('fsdp')
- up_updated: float32 [768, 3072], P('fsdp')
- down_updated: float32 [3072, 768], P('fsdp')
- mod_updated: float32 [128, 4608], P(None, 'fsdp')
- qkv_moment: float32 [768, 2304], P('fsdp')
- out_moment: float32 [768, 768], P('fsdp')
- up_moment: float32 [768, 3072], P('fsdp')
- down_moment: float32 [3072, 768], P('fsdp')
- mod_moment: float32 [128, 4608], P(None, 'fsdp')
- qkv_variance: float32 [768, 2304], P('fsdp')
- out_variance: float32 [768, 768], P('fsdp')
- up_variance: float32 [768, 3072], P('fsdp')
- down_variance: float32 [3072, 768], P('fsdp')
- mod_variance: float32 [128, 4608], P(None, 'fsdp')
- vectors_updated: float32 [9984], P('fsdp')
- vectors_moment: float32 [9984], P('fsdp')
- vectors_variance: float32 [9984], P('fsdp')
- weight_norms: float32 [2, 5], replicated
Inputs may be any that keep to these rules, and one draw needn't show every extreme that they name: `seg_sizes`: in every row the nonzero entries come first, each is 1024, 512 or 128, and they sum to 1024; the rest are zero. `seq_lengths`: each entry lies between half of the matching seg_sizes entry and all of it; zero where that entry is zero.
All inputs are finite; a program needn't handle non-finite values. No bound on the sum of `absorbed` on one device may be relied on, other than what follows from the above.
Results may differ from a plain program's by a relative error of at most 0.025.
The roundings to bfloat16 on the way count: a program that leaves them out, or rounds other values in their place, can miss the bound.
Values may be sent and summed in bfloat16 or wider, within the bound.
No kernel may reach another device: no remote copies, remote signals or barrier semaphores. Data moves between devices by JAX's collectives and lax.ppermute only.
A program may use at most 320 MiB of HBM per device.

v0:
```python
import functools
import math

import jax
import jax.numpy as jnp
from jax import lax
from jax.sharding import PartitionSpec as P

D = 768
HEADS = 12
HDIM = 64
FF = 3072
COND = 128
SLOTS = 1024
NSEG = 8
QBLOCK = 512
STEP = 10


BETA_ONE = 0.9
BETA_TWO = 0.999
EPSILON = 1e-06
DECAY_RATE = 0.01
MATRIX_RATE = 0.3
VECTOR_RATE = 1.0


def linear(left_side, right_side):
    return jnp.dot(left_side, right_side, preferred_element_type=jnp.float32)


def precise(left_side, right_side):
    return jnp.dot(
        left_side, right_side, precision=lax.Precision.HIGHEST, preferred_element_type=jnp.float32
    )


def product(pattern, left_side, right_side):
    return jnp.einsum(pattern, left_side, right_side, preferred_element_type=jnp.float32)


def normalize(values):
    average = jnp.mean(values, axis=-1, keepdims=True)
    centered = values - average
    return centered * lax.rsqrt(jnp.mean(centered * centered, axis=-1, keepdims=True) + 1e-05)


def modulate(values, gain_in, shift_in, scale_in):
    return normalize(values) * gain_in * (1.0 + scale_in) + shift_in


def rotate(values, position):
    half_dim = values.shape[-1] // 2
    inverse = jnp.exp(jnp.arange(half_dim, dtype=jnp.float32) * (-math.log(10000.0) / half_dim))
    angles = position.astype(jnp.float32)[:, None] * inverse[None, :]
    cosine = jnp.cos(angles)[:, None, :]
    sine_of = jnp.sin(angles)[:, None, :]
    leading = values[..., :half_dim]
    trailing = values[..., half_dim:]
    return jnp.concatenate(
        [leading * cosine - trailing * sine_of, trailing * cosine + leading * sine_of], axis=-1
    )


def layout_tables(sizes_row, lengths_row):
    slot_ids = jnp.arange(sizes_row.shape[0] * 0 + SLOTS, dtype=jnp.int32)
    seg_ends = jnp.cumsum(sizes_row)
    starts = seg_ends - sizes_row
    segment = jnp.sum((slot_ids[:, None] >= seg_ends[None, :]).astype(jnp.int32), axis=1)
    member = segment[:, None] == jnp.arange(NSEG, dtype=jnp.int32)[None, :]
    offset = jnp.sum(jnp.where(member, starts[None, :], 0), axis=1)
    length_of = jnp.sum(jnp.where(member, lengths_row[None, :], 0), axis=1)
    position = slot_ids - offset
    return (segment, member, position, position < length_of)


def condition(steps_row):
    half_cond = COND // 2
    frequency = jnp.exp(jnp.arange(half_cond, dtype=jnp.float32) * (-math.log(10000.0) / half_cond))
    angles = steps_row.astype(jnp.float32)[:, None] * frequency[None, :]
    return jax.nn.silu(jnp.concatenate([jnp.cos(angles), jnp.sin(angles)], axis=1))


def split_vectors(vector_all):
    return (
        vector_all[:D],
        vector_all[D : 2 * D],
        vector_all[2 * D : 2 * D + FF],
        vector_all[2 * D + FF : 3 * D + FF],
        vector_all[3 * D + FF :],
    )


def block_scores(block_query, key_low, block_segment, segment, valid_slot, scale_by):
    allowed = (block_segment[:, None] == segment[None, :]) & valid_slot[None, :]
    return jnp.where(allowed[None], product("qhd,khd->hqk", block_query, key_low) * scale_by, -1e30)


def row_pass(packed, weights_full):
    row_inputs, row_cot, sizes_row, lengths_row, steps_row, marks_row = packed
    qkv_low, out_low, up_low, down_low, mod_low, vector_low = weights_full
    gain_one, gain_two, bias_up, bias_down, bias_mod = split_vectors(vector_low.astype(jnp.float32))
    segment, member, position, valid_slot = layout_tables(sizes_row, lengths_row)
    members = member.astype(jnp.float32)
    condition_low = condition(steps_row).astype(jnp.bfloat16)
    modulation = linear(condition_low, mod_low) + bias_mod
    per_slot = precise(members, modulation)
    shift_one, scale_one, gate_one, shift_two, scale_two, gate_two = jnp.split(per_slot, 6, axis=1)
    inputs_wide = row_inputs.astype(jnp.float32)
    first_norm, first_back = jax.vjp(modulate, inputs_wide, gain_one, shift_one, scale_one)
    first_low = first_norm.astype(jnp.bfloat16)
    mixed_qkv = linear(first_low, qkv_low)
    slots_count = row_inputs.shape[0]
    heads_shape = (slots_count, HEADS, HDIM)
    turner = functools.partial(rotate, position=position)
    query_turned, query_back = jax.vjp(turner, mixed_qkv[:, :D].reshape(heads_shape))
    key_turned, key_back = jax.vjp(turner, mixed_qkv[:, D : 2 * D].reshape(heads_shape))
    query_low = query_turned.astype(jnp.bfloat16)
    key_low = key_turned.astype(jnp.bfloat16)
    value_low = mixed_qkv[:, 2 * D :].reshape(heads_shape).astype(jnp.bfloat16)
    scale_by = HDIM ** (-0.5)
    attended_parts = []
    peaks = []
    totals = []
    for begin_at in range(0, slots_count, QBLOCK):
        block_query = query_low[begin_at : begin_at + QBLOCK]
        masked = block_scores(
            block_query,
            key_low,
            segment[begin_at : begin_at + QBLOCK],
            segment,
            valid_slot,
            scale_by,
        )
        row_peak = jnp.max(masked, axis=-1, keepdims=True)
        weights_exp = jnp.exp(masked - row_peak)
        row_total = jnp.sum(weights_exp, axis=-1, keepdims=True)
        chances = (weights_exp / row_total).astype(jnp.bfloat16)
        attended_parts.append(product("hqk,khd->qhd", chances, value_low))
        peaks.append(row_peak)
        totals.append(row_total)
    attended_low = (
        jnp.concatenate(attended_parts, axis=0).reshape(slots_count, D).astype(jnp.bfloat16)
    )
    branch = linear(attended_low, out_low)
    middle = inputs_wide + gate_one * branch
    second_norm, second_back = jax.vjp(modulate, middle, gain_two, shift_two, scale_two)
    second_low = second_norm.astype(jnp.bfloat16)
    up_values = linear(second_low, up_low) + bias_up
    hidden_wide, gelu_back = jax.vjp(functools.partial(jax.nn.gelu, approximate=True), up_values)
    hidden_low = hidden_wide.astype(jnp.bfloat16)
    feed_out = linear(hidden_low, down_low) + bias_down
    out_hidden = middle + gate_two * feed_out
    weight_mask = (marks_row * valid_slot.astype(jnp.int32)).astype(jnp.float32)
    grad_out = row_cot.astype(jnp.float32) * weight_mask[:, None]
    grad_mlp = (grad_out * gate_two).astype(jnp.bfloat16)
    grad_gate_two = grad_out * feed_out
    grad_down = linear(hidden_low.T, grad_mlp)
    grad_hidden = linear(grad_mlp, down_low.T)
    (grad_up_wide,) = gelu_back(grad_hidden)
    grad_up = grad_up_wide.astype(jnp.bfloat16)
    grad_up_weight = linear(second_low.T, grad_up)
    grad_second = linear(grad_up, up_low.T)
    grad_middle_norm, grad_gain_two, grad_shift_two, grad_scale_two = second_back(grad_second)
    grad_middle = grad_out + grad_middle_norm
    grad_gate_one = grad_middle * branch
    grad_branch = (grad_middle * gate_one).astype(jnp.bfloat16)
    grad_attn_out = linear(attended_low.T, grad_branch)
    grad_attended = linear(grad_branch, out_low.T).astype(jnp.bfloat16).reshape(heads_shape)
    grad_query_parts = []
    grad_key = jnp.zeros(heads_shape, jnp.float32)
    grad_value = jnp.zeros(heads_shape, jnp.float32)
    for number, begin_at in enumerate(range(0, slots_count, QBLOCK)):
        block_query = query_low[begin_at : begin_at + QBLOCK]
        masked = block_scores(
            block_query,
            key_low,
            segment[begin_at : begin_at + QBLOCK],
            segment,
            valid_slot,
            scale_by,
        )
        chances_wide = jnp.exp(masked - peaks[number]) / totals[number]
        chances_low = chances_wide.astype(jnp.bfloat16)
        block_grad = grad_attended[begin_at : begin_at + QBLOCK]
        grad_chances = product("qhd,khd->hqk", block_grad, value_low)
        delta_row = jnp.sum(chances_wide * grad_chances, axis=-1, keepdims=True)
        grad_scores = (chances_wide * (grad_chances - delta_row) * scale_by).astype(jnp.bfloat16)
        grad_query_parts.append(product("hqk,khd->qhd", grad_scores, key_low))
        grad_key = grad_key + product("hqk,qhd->khd", grad_scores, block_query)
        grad_value = grad_value + product("hqk,qhd->khd", chances_low, block_grad)
    (grad_query,) = query_back(jnp.concatenate(grad_query_parts, axis=0))
    (grad_key_turned,) = key_back(grad_key)
    grad_mixed = jnp.concatenate(
        [
            grad_query.reshape(slots_count, D),
            grad_key_turned.reshape(slots_count, D),
            grad_value.reshape(slots_count, D),
        ],
        axis=1,
    ).astype(jnp.bfloat16)
    grad_qkv = linear(first_low.T, grad_mixed)
    grad_first = linear(grad_mixed, qkv_low.T)
    grad_inputs_norm, grad_gain_one, grad_shift_one, grad_scale_one = first_back(grad_first)
    grad_in = grad_middle + grad_inputs_norm
    grad_slot = jnp.concatenate(
        [
            grad_shift_one,
            grad_scale_one,
            grad_gate_one,
            grad_shift_two,
            grad_scale_two,
            grad_gate_two,
        ],
        axis=1,
    )
    grad_modulation = precise(members.T, grad_slot)
    grad_mod = precise(condition_low.astype(jnp.float32).T, grad_modulation)
    grad_vectors = jnp.concatenate(
        [
            grad_gain_one,
            grad_gain_two,
            jnp.sum(grad_up.astype(jnp.float32), axis=0),
            jnp.sum(grad_mlp.astype(jnp.float32), axis=0),
            jnp.sum(grad_modulation, axis=0),
        ]
    )
    return (
        out_hidden,
        grad_in,
        (grad_qkv, grad_attn_out, grad_up_weight, grad_down, grad_mod, grad_vectors),
    )


def adam_direction(weight, first_old, second_old, gradient, decay_rate):
    first_new = BETA_ONE * first_old + (1.0 - BETA_ONE) * gradient
    second_new = BETA_TWO * second_old + (1.0 - BETA_TWO) * gradient * gradient
    direction = (
        first_new
        / (1.0 - BETA_ONE**STEP)
        / (jnp.sqrt(second_new / (1.0 - BETA_TWO**STEP)) + EPSILON)
        + decay_rate * weight
    )
    return (first_new, second_new, direction)


def directions(weights_in, firsts_in, seconds_in, grads_in):
    results = []
    weight_squares = []
    update_squares = []
    for number in range(6):
        decay_rate = DECAY_RATE if number < 5 else 0.0
        first_new, second_new, direction = adam_direction(
            weights_in[number], firsts_in[number], seconds_in[number], grads_in[number], decay_rate
        )
        results.append((first_new, second_new, direction))
        if number < 5:
            weight_squares.append(jnp.sum(weights_in[number] * weights_in[number]))
            update_squares.append(jnp.sum(direction * direction))
    return (results, jnp.stack([jnp.stack(weight_squares), jnp.stack(update_squares)]))


def finish(weights_in, results, summed):
    norm_roots = jnp.sqrt(summed)
    renewed = []
    for number in range(5):
        trust_ratio = norm_roots[0, number] / (norm_roots[1, number] + EPSILON)
        renewed.append(weights_in[number] - MATRIX_RATE * trust_ratio * results[number][2])
    renewed.append(weights_in[5] - VECTOR_RATE * results[5][2])
    return (renewed, norm_roots)


def on_device(
    inputs,
    cotangent,
    seg_sizes,
    seq_lengths,
    timesteps,
    absorbed,
    qkv_weight,
    out_weight,
    up_weight,
    down_weight,
    mod_weight,
    qkv_first,
    out_first,
    up_first,
    down_first,
    mod_first,
    qkv_second,
    out_second,
    up_second,
    down_second,
    mod_second,
    vectors,
    vectors_first,
    vectors_second,
):
    masters = (qkv_weight, out_weight, up_weight, down_weight, mod_weight, vectors)
    firsts = (qkv_first, out_first, up_first, down_first, mod_first, vectors_first)
    seconds = (qkv_second, out_second, up_second, down_second, mod_second, vectors_second)
    sent = tuple((master.astype(jnp.bfloat16) for master in masters))
    gathered = (
        lax.all_gather(sent[0], "fsdp", axis=0, tiled=True),
        lax.all_gather(sent[1], "fsdp", axis=0, tiled=True),
        lax.all_gather(sent[2], "fsdp", axis=0, tiled=True),
        lax.all_gather(sent[3], "fsdp", axis=0, tiled=True),
        lax.all_gather(sent[4], "fsdp", axis=1, tiled=True),
        lax.all_gather(sent[5], "fsdp", axis=0, tiled=True),
    )
    rows_all = (inputs, cotangent, seg_sizes, seq_lengths, timesteps, absorbed)
    zero_grads = tuple((jnp.zeros(weight.shape, jnp.float32) for weight in gathered))

    def grad_step(weights_full):

        def one_step(running, packed):
            out_row, grad_in, grads = row_pass(packed, weights_full)
            return (jax.tree.map(jnp.add, running, grads), (out_row.astype(jnp.bfloat16), grad_in))

        return one_step

    summed_grads, (out_rows, grad_rows) = lax.scan(grad_step(gathered), zero_grads, rows_all)
    shard_grads = (
        lax.psum_scatter(summed_grads[0], "fsdp", scatter_dimension=0, tiled=True),
        lax.psum_scatter(summed_grads[1], "fsdp", scatter_dimension=0, tiled=True),
        lax.psum_scatter(summed_grads[2], "fsdp", scatter_dimension=0, tiled=True),
        lax.psum_scatter(summed_grads[3], "fsdp", scatter_dimension=0, tiled=True),
        lax.psum_scatter(summed_grads[4], "fsdp", scatter_dimension=1, tiled=True),
        lax.psum_scatter(summed_grads[5], "fsdp", scatter_dimension=0, tiled=True),
    )
    group_grads = (
        lax.psum(shard_grads[0].astype(jnp.bfloat16), "rep").astype(jnp.float32),
        lax.psum(shard_grads[1].astype(jnp.bfloat16), "rep").astype(jnp.float32),
        lax.psum(shard_grads[2].astype(jnp.bfloat16), "rep").astype(jnp.float32),
        lax.psum(shard_grads[3].astype(jnp.bfloat16), "rep").astype(jnp.float32),
        lax.psum(shard_grads[4].astype(jnp.bfloat16), "rep").astype(jnp.float32),
        lax.psum(shard_grads[5].astype(jnp.bfloat16), "rep").astype(jnp.float32),
    )
    results, squares = directions(masters, firsts, seconds, group_grads)
    summed = lax.psum(squares, "fsdp")
    renewed, norm_roots = finish(masters, results, summed)
    firsts_new = [record[0] for record in results]
    seconds_new = [record[1] for record in results]
    return (
        out_rows,
        grad_rows,
        renewed[0],
        renewed[1],
        renewed[2],
        renewed[3],
        renewed[4],
        firsts_new[0],
        firsts_new[1],
        firsts_new[2],
        firsts_new[3],
        firsts_new[4],
        seconds_new[0],
        seconds_new[1],
        seconds_new[2],
        seconds_new[3],
        seconds_new[4],
        renewed[5],
        firsts_new[5],
        seconds_new[5],
        norm_roots,
    )


def solution(mesh):
    placed = (
        P(("rep", "fsdp"), None, None),
        P(("rep", "fsdp"), None, None),
        P(("rep", "fsdp"), None),
        P(("rep", "fsdp"), None),
        P(("rep", "fsdp"), None),
        P(("rep", "fsdp"), None),
        P("fsdp", None),
        P("fsdp", None),
        P("fsdp", None),
        P("fsdp", None),
        P(None, "fsdp"),
        P("fsdp", None),
        P("fsdp", None),
        P("fsdp", None),
        P("fsdp", None),
        P(None, "fsdp"),
        P("fsdp", None),
        P("fsdp", None),
        P("fsdp", None),
        P("fsdp", None),
        P(None, "fsdp"),
        P("fsdp"),
        P("fsdp"),
        P("fsdp"),
    )
    return jax.shard_map(
        on_device,
        mesh=mesh,
        in_specs=placed,
        out_specs=(
            P(("rep", "fsdp"), None, None),
            P(("rep", "fsdp"), None, None),
            P("fsdp", None),
            P("fsdp", None),
            P("fsdp", None),
            P("fsdp", None),
            P(None, "fsdp"),
            P("fsdp", None),
            P("fsdp", None),
            P("fsdp", None),
            P("fsdp", None),
            P(None, "fsdp"),
            P("fsdp", None),
            P("fsdp", None),
            P("fsdp", None),
            P("fsdp", None),
            P(None, "fsdp"),
            P("fsdp"),
            P("fsdp"),
            P("fsdp"),
            P(),
        ),
        check_vma=False,
    )
```

profile of v0, /device:TPU:0, one launch (start us, length us, event | category | flops | bytes accessed | tf_op | source)
XLA Modules:
  0.0 1461.7 jit_solution(8171032554426275306)
XLA Ops:
  17.8 78.8 %all-reduce.4 = bf16[9984]{0:T(1024)(128)(2,1)S(1)} all-reduce(bf16[9984]{0:T(1024)(128)(2,1)S(1)} %dynamic-update-slice), channel_id=1, replica_groups=mesh['rep'=2,'fsdp'=16] {'fsdp'}, use_global_device_ids=true, to_apply=%add.4 | all-reduce | flops 9984 | bytes 39936
  119.3 24.6 %all-gather.8.cloned.1.call-done = bf16[768,2304]{1,0:T(8,128)(2,1)} async-done(((bf16[48,2304]{1,0:T(8,128)(2,1)}), bf16[768,2304]{1,0:T(8,128)(2,1)}) %all-gather.8.cloned.1.call-update) | async-done | bytes 3538960 | tf_op jit(solution)/shard_map/all_gather | solution.py:304
  175.6 14.6 fusion.167
  190.2 10.7 fusion.92
  201.0 33.3 %fusion.166 = (f32[12,512]{1,0:T(8,128)S(1)}, f32[12,512,1024]{2,1,0:T(8,128)}) fusion(f32[12,512,1024]{2,1,0:T(8,128)} %fusion.106, pred[512,1024]{1,0:T(8,128)(4,1)S(1)} %copy-done.46), kind=kOutput, calls=%fused_computation.240 | output fusion | flops 37749760 | bytes 50880512 | tf_op jit(solution)/shard_map/while/body/eval_jaxpr/sub | solution.py:136
  234.2 10.4 fusion.89
  261.1 23.5 %all-gather.12.cloned.1.call-done = bf16[768,3072]{1,0:T(8,128)(2,1)} async-done(((bf16[48,3072]{1,0:T(8,128)(2,1)}), bf16[768,3072]{1,0:T(8,128)(2,1)}) %all-gather.12.cloned.1.call-update) | async-done | bytes 4718608 | tf_op jit(solution)/shard_map/all_gather | solution.py:306
  284.6 13.3 multiply_convert_fusion.2
  297.9 69.1 %all-gather.14.cloned.1.call-done = bf16[3072,768]{1,0:T(8,128)(2,1)} async-done(((bf16[192,768]{1,0:T(8,128)(2,1)}), bf16[3072,768]{1,0:T(8,128)(2,1)}) %all-gather.14.cloned.1.call-update) | async-done | bytes 4718608 | tf_op jit(solution)/shard_map/all_gather | solution.py:307
  366.9 18.6 %convert_reduce_fusion = (f32[3072]{0:T(1024)}, bf16[1024,3072]{1,0:T(8,128)(2,1)}) fusion(f32[1024,3072]{1,0:T(8,128)} %get-tuple-element.182, f32[3072]{0:T(1024)S(1)} %copy-done.84, bf16[1024,768]{1,0:T(8,128)(2,1)} %get-tuple-element.111, bf16[3072,768]{1,0:T(8,128)(2,1)} %all-gather.14.cloned.1.call-done), kind=kOutput, calls=%fused_computation.25 | convolution fusion | flops 4904186880 | bytes 25190400 | tf_op jit(solution)/shard_map/while/body/eval_jaxpr/dot_general | solution.py:29
  394.8 10.3 fusion.174
  426.8 43.3 %fusion.80 = f32[512,12,64]{0,2,1:T(8,128)} fusion(f32[12,512,1024]{2,1,0:T(8,128)} %fusion.175, bf16[1024,12,32]{0,2,1:T(8,128)(2,1)} %copy-done.25, bf16[1024,12,32]{0,2,1:T(8,128)(2,1)} %copy-done.23, f32[12,512,1024]{2,1,0:T(8,128)} %get-tuple-element.178, f32[12,512]{1,0:T(8,128)S(1)} %get-tuple-element.177), kind=kOutput, calls=%fused_computation.118 | convolution fusion | flops 852499456 | bytes 53501952 | tf_op jit(solution)/shard_map/while/body/eval_jaxpr/hqk,khd->qhd/dot_general | solution.py:39
  470.1 44.9 %fusion.24 = f32[12,64,1024]{2,1,0:T(8,128)} fusion(f32[12,512,1024]{2,1,0:T(8,128)} %fusion.175, bf16[1024,12,32]{0,2,1:T(8,128)(2,1)} %copy-done.22, bf16[1024,12,32]{0,2,1:T(8,128)(2,1)} %copy-done.21, f32[12,512,1024]{2,1,0:T(8,128)} %get-tuple-element.178, f32[12,512]{1,0:T(8,128)S(1)} %get-tuple-element.177), kind=kOutput, calls=%fused_computation.35 | convolution fusion | flops 850926592 | bytes 105447424 | tf_op jit(solution)/shard_map/while/body/eval_jaxpr/hqk,qhd->khd/dot_general | solution.py:39
  515.0 11.3 fusion.37
  536.5 12.4 add_convert_fusion
  549.0 50.1 %fusion.77 = f32[512,12,64]{0,2,1:T(8,128)} fusion(f32[12,512,1024]{2,1,0:T(8,128)} %fusion.176, bf16[1024,12,32]{0,2,1:T(8,128)(2,1)S(1)} %copy-done.26, bf16[1024,12,32]{0,2,1:T(8,128)(2,1)S(1)} %copy-done.24, f32[12,512,1024]{2,1,0:T(8,128)} %get-tuple-element.176, f32[12,512]{1,0:T(8,128)S(1)} %copy-done.94), kind=kOutput, calls=%fused_computation.117 | convolution fusion | flops 852499456 | bytes 53501952 | tf_op jit(solution)/shard_map/while/body/eval_jaxpr/hqk,khd->qhd/dot_general | solution.py:39
  599.1 44.6 %add_bitcast_fusion.1 = f32[1024,12,64]{0,2,1:T(8,128)S(1)} fusion(f32[12,64,1024]{2,1,0:T(8,128)} %fusion.24, f32[12,512,1024]{2,1,0:T(8,128)} %fusion.176, bf16[1024,12,32]{0,2,1:T(8,128)(2,1)} %copy-done.21, bf16[1024,12,32]{0,2,1:T(8,128)(2,1)} %copy-done.22, f32[12,512,1024]{2,1,0:T(8,128)} %get-tuple-element.176, f32[12,512]{1,0:T(8,128)S(1)} %copy-done.94), kind=kOutput, calls=%fused_computation.89 | convolution fusion | flops 851713024 | bytes 58220544 | tf_op jit(solution)/shard_map/while/body/eval_jaxpr/hqk,qhd->khd/dot_general | solution.py:39
  702.7 10.3 fusion.178
  715.0 92.6 %reduce-scatter.14.cloned.1.call-done = f32[128,288]{0,1:T(8,128)} async-done(((f32[128,4608]{0,1:T(8,128)}), f32[128,288]{0,1:T(8,128)}) %reduce-scatter.14.cloned.1.call-update) | async-done | bytes 147472 | tf_op jit(solution)/shard_map/reduce_scatter | solution.py:328
  809.2 154.4 %reduce-scatter.6.cloned.1.call-done = f32[48,2304]{1,0:T(8,128)} async-done(((f32[768,2304]{1,0:T(8,128)}), f32[48,2304]{1,0:T(8,128)}) %reduce-scatter.6.cloned.1.call-update) | async-done | bytes 442384 | tf_op jit(solution)/shard_map/reduce_scatter | solution.py:324
  965.3 173.7 %reduce-scatter.12.cloned.1.call-done = f32[192,768]{1,0:T(8,128)} async-done(((f32[3072,768]{1,0:T(8,128)}), f32[192,768]{1,0:T(8,128)}) %reduce-scatter.12.cloned.1.call-update) | async-done | bytes 589840 | tf_op jit(solution)/shard_map/reduce_scatter | solution.py:327
  1140.8 174.5 %reduce-scatter.10.cloned.1.call-done = f32[48,3072]{1,0:T(8,128)} async-done(((f32[768,3072]{1,0:T(8,128)}), f32[48,3072]{1,0:T(8,128)}) %reduce-scatter.10.cloned.1.call-update) | async-done | bytes 589840 | tf_op jit(solution)/shard_map/reduce_scatter | solution.py:326
  1317.3 20.4 %all-reduce.10.cloned.1.call-done = (bf16[48,2304]{1,0:T(8,128)(2,1)}, bf16[48,768]{1,0:T(8,128)(2,1)}, bf16[48,3072]{1,0:T(8,128)(2,1)}, bf16[192,768]{1,0:T(8,128)(2,1)}, bf16[128,288]{0,1:T(8,128)(2,1)}) async-done(((bf16[48,2304]{1,0:T(8,128)(2,1)}, bf16[48,768]{1,0:T(8,128)(2,1)}, bf16[48,3072]{1,0:T(8,128)(2,1)}, bf16[192,768]{1,0:T(8,128)(2,1)}, bf16[128,288]{0,1:T(8,128)(2,1)}), ...) | async-done | bytes 958480 | tf_op jit(solution)/shard_map/psum | solution.py:332
  1357.0 78.4 %all-reduce.6 = (f32[2,5]{1,0:T(2,128)S(1)}, bf16[9984]{0:T(1024)(128)(2,1)}) all-reduce(f32[2,5]{1,0:T(2,128)S(1)} %pad_maximum_fusion.10, f32[9984]{0:T(1024)} %copy-done.70), channel_id=1, replica_groups=mesh['rep'=2,'fsdp'=16] {'fsdp'}, use_global_device_ids=true, to_apply=%region_38.39 | all-reduce | flops 9994 | bytes 59984 | tf_op jit(solution)/shard_map/psum | solution.py:340
  (326 shorter events, 220.4 us)
Async XLA Ops:
  7.2 94.7 %all-gather.6.cloned.1.call-start = ((), (), s32[]{:S(2)}) async-start(), calls=%async_computation.5 | async-start | bytes 1253376 | tf_op jit(solution)/shard_map/all_gather | solution.py:308
  9.0 134.9 %all-gather.8.cloned.1.call-start = ((), (), s32[]{:S(2)}) async-start(), calls=%async_computation.6 | async-start | bytes 3760128 | tf_op jit(solution)/shard_map/all_gather | solution.py:304
  10.8 235.2 %all-gather.10.cloned.1.call-start = ((), (), s32[]{:S(2)}) async-start(), calls=%async_computation.7 | async-start | bytes 1253376 | tf_op jit(solution)/shard_map/all_gather | solution.py:305
  12.4 272.2 %all-gather.12.cloned.1.call-start = ((), (), s32[]{:S(2)}) async-start(), calls=%async_computation.8 | async-start | bytes 5013504 | tf_op jit(solution)/shard_map/all_gather | solution.py:306
  14.3 352.6 %all-gather.14.cloned.1.call-start = ((), (), s32[]{:S(2)}) async-start(), calls=%async_computation.9 | async-start | bytes 5013504 | tf_op jit(solution)/shard_map/all_gather | solution.py:307
  16.2 697.1 %reduce-scatter.8.cloned.1.call-start = ((), (), s32[]{:S(2)}) async-start(), calls=%async_computation.11 | async-start | bytes 2506752 | tf_op jit(solution)/shard_map/reduce_scatter | solution.py:325
  97.9 307.2 %copy-start.68 = (f32[768]{0:T(1024)}, f32[768]{0:T(1024)S(1)}, u32[]{:S(2)}) copy-start(f32[768]{0:T(1024)S(1)} %get-tuple-element.152) | copy-start | bytes 9220
  99.7 308.8 %copy-start.63 = (f32[1024]{0:T(1024)}, f32[1024]{0:T(1024)S(1)}, u32[]{:S(2)}) copy-start(f32[1024]{0:T(1024)S(1)} %get-tuple-element.126) | copy-start | bytes 12292
  536.5 271.1 %reduce-scatter.14.cloned.1.call-start = ((), (), s32[]{:S(2)}) async-start(), calls=%async_computation.14 | async-start | bytes 2506752 | tf_op jit(solution)/shard_map/reduce_scatter | solution.py:328
  680.7 282.9 %reduce-scatter.6.cloned.1.call-start = ((), (), s32[]{:S(2)}) async-start(), calls=%async_computation.10 | async-start | bytes 7520256 | tf_op jit(solution)/shard_map/reduce_scatter | solution.py:324
  689.7 449.4 %reduce-scatter.12.cloned.1.call-start = ((), (), s32[]{:S(2)}) async-start(), calls=%async_computation.13 | async-start | bytes 10027008 | tf_op jit(solution)/shard_map/reduce_scatter | solution.py:327
  701.3 614.0 %reduce-scatter.10.cloned.1.call-start = ((), (), s32[]{:S(2)}) async-start(), calls=%async_computation.12 | async-start | bytes 10027008 | tf_op jit(solution)/shard_map/reduce_scatter | solution.py:326
  713.1 604.2 %copy-start.85 = (f32[768]{0:T(1024)S(1)}, f32[768]{0:T(1024)}, u32[]{:S(2)}) copy-start(f32[768]{0:T(1024)} %get-tuple-element.84) | copy-start | bytes 9220
  713.1 604.2 %copy-start.83 = (f32[3072]{0:T(1024)S(1)}, f32[3072]{0:T(1024)}, u32[]{:S(2)}) copy-start(f32[3072]{0:T(1024)} %get-tuple-element.185) | copy-start | bytes 36868
  713.1 604.2 %copy-start.82 = (f32[768]{0:T(1024)S(1)}, f32[768]{0:T(1024)}, u32[]{:S(2)}) copy-start(f32[768]{0:T(1024)} %get-tuple-element.110) | copy-start | bytes 9220
  713.1 604.2 %copy-start.65 = (f32[4608]{0:T(1024)S(1)}, f32[4608]{0:T(1024)}, u32[]{:S(2)}) copy-start(f32[4608]{0:T(1024)} %get-tuple-element.187) | copy-start | bytes 55300
  713.1 624.7 %copy-start.37 = (f32[48,768]{1,0:T(8,128)S(1)}, f32[48,768]{1,0:T(8,128)}, u32[]{:S(2)}) copy-start(f32[48,768]{1,0:T(8,128)} %param.31) | copy-start | bytes 442372
  713.1 624.7 %copy-start.53 = (f32[48,768]{1,0:T(8,128)S(1)}, f32[48,768]{1,0:T(8,128)}, u32[]{:S(2)}) copy-start(f32[48,768]{1,0:T(8,128)} %param.36) | copy-start | bytes 442372
  713.1 624.7 %copy-start.54 = (f32[48,768]{1,0:T(8,128)S(1)}, f32[48,768]{1,0:T(8,128)}, u32[]{:S(2)}) copy-start(f32[48,768]{1,0:T(8,128)} %param.41) | copy-start | bytes 442372
  713.1 627.0 %copy-start.36 = (f32[128,288]{0,1:T(8,128)S(1)}, f32[128,288]{0,1:T(8,128)}, u32[]{:S(2)}) copy-start(f32[128,288]{0,1:T(8,128)} %param.34) | copy-start | bytes 442372
  713.1 629.7 %copy-start.20 = (f32[48,2304]{1,0:T(8,128)S(1)}, f32[48,2304]{1,0:T(8,128)}, u32[]{:S(2)}) copy-start(f32[48,2304]{1,0:T(8,128)} %param.30) | copy-start | bytes 1327108
  713.2 629.7 %copy-start.47 = (f32[48,2304]{1,0:T(8,128)S(1)}, f32[48,2304]{1,0:T(8,128)}, u32[]{:S(2)}) copy-start(f32[48,2304]{1,0:T(8,128)} %param.35) | copy-start | bytes 1327108
  713.2 629.7 %copy-start.48 = (f32[48,2304]{1,0:T(8,128)S(1)}, f32[48,2304]{1,0:T(8,128)}, u32[]{:S(2)}) copy-start(f32[48,2304]{1,0:T(8,128)} %param.40) | copy-start | bytes 1327108
  713.2 624.6 %all-reduce.10.cloned.1.call-start = ((), (), s32[]{:S(2)}) async-start(), calls=%async_computation.15 | async-start | bytes 1916928 | tf_op jit(solution)/shard_map/psum | solution.py:332
  (87 other events, 2599.7 us)
Sparse Core Ops, SparseCore 0:
  11.5 59.0 all-gather.5
  73.9 69.9 all-gather.7
  147.3 54.6 all-gather.9
  205.2 79.3 all-gather.11
  287.8 79.0 all-gather.13
  536.6 127.5 reduce-scatter.7
  680.8 126.7 reduce-scatter.13
  812.9 150.6 reduce-scatter.5
  969.3 169.7 reduce-scatter.11
  1145.5 169.8 reduce-scatter.9
  1319.2 18.5 all-reduce.9
where the time goes:
time: 1470 us; the launch traced here: 1460 us
  waiting for transfers between devices  733 us (50%)
  matrix products  397 us (27%)
  blocking collectives  160 us (11%)
  other arithmetic  106 us (7%)
  local copies, waits for them, and re-layouts  41.9 us (3%)
  between operations  23 us (2%)
    dot_general x11, matrix products, product(): jnp.einsum(pattern, left_side, right_side, preferred_element_type=jnp.flo...  258 us
    reduce_scatter x1, waiting for transfers between devices, on_device(): lax.psum_scatter(summed_grads[2], 'fsdp', scatter_dimension=0, tiled=True)  175 us
    reduce_scatter x1, waiting for transfers between devices, on_device(): lax.psum_scatter(summed_grads[3], 'fsdp', scatter_dimension=0, tiled=True)  174 us
    reduce_scatter x1, waiting for transfers between devices, on_device(): lax.psum_scatter(summed_grads[0], 'fsdp', scatter_dimension=0, tiled=True)  154 us
    dot_general x13, matrix products, linear(): return jnp.dot(left_side, right_side, preferred_element_type=jnp.float32)  106 us
    reduce_scatter x1, waiting for transfers between devices, on_device(): lax.psum_scatter(summed_grads[4], 'fsdp', scatter_dimension=1, tiled=True)  92.6 us
    unnamed x1, blocking collectives  78.8 us
    psum x1, blocking collectives, on_device(): summed = lax.psum(squares, 'fsdp')  78.4 us
  transfers between devices with their start and end apart: 11, of which 8 were waited for; matrix products, arithmetic and copies ran while one was open for 22% of the time, Pallas kernels for 0%

commit v1 on v0

v1 whole, which is shorter than its diff:
```python
import functools
import math

import jax
import jax.numpy as jnp
import numpy as np
from jax import lax
from jax.experimental import pallas as pl
from jax.experimental.pallas import tpu as pltpu
from jax.sharding import PartitionSpec as P

D = 768
HEADS = 12
HDIM = 64
FF = 3072
COND = 128
SLOTS = 1024
NSEG = 8
STEP = 10
TILE = 128
BLOCKS = SLOTS // TILE

BETA_ONE = 0.9
BETA_TWO = 0.999
EPSILON = 1e-06
DECAY_RATE = 0.01
MATRIX_RATE = 0.3
VECTOR_RATE = 1.0

PAIR = 128
NT = (((1,), (1,)), ((), ()))
NN = (((1,), (0,)), ((), ()))
TN = (((0,), (0,)), ((), ()))
BF = jnp.bfloat16
F32 = jnp.float32


def mm(a, b, dims=NN):
    return lax.dot_general(a, b, dims, preferred_element_type=F32)


def swap_halves(v):
    lane = lax.broadcasted_iota(jnp.int32, v.shape, 1)
    return jnp.where(lane % 64 < 32, pltpu.roll(v, PAIR - 32, 1), pltpu.roll(v, 32, 1))


def attention_forward_kernel(block, q_ref, k_ref, v_ref, cos_ref, sin_ref, fq_ref, fk_ref,
                             o_ref, qr_ref, kr_ref, vr_ref, fo_ref, ka, kb, va, vb):
    slots = q_ref.shape[0]
    low_all = lax.broadcasted_iota(jnp.int32, (slots, PAIR), 1) < 64
    cos, sin = cos_ref[...], sin_ref[...]
    q = q_ref[...]
    k = k_ref[...]
    qr_ref[...] = ((q * cos + swap_halves(q) * sin) * 0.125).astype(BF)
    k_low = (k * cos + swap_halves(k) * sin).astype(BF)
    v_low = v_ref[...].astype(BF)
    kr_ref[...] = k_low
    vr_ref[...] = v_low
    fk = fk_ref[...]
    one = jnp.ones((slots, PAIR), BF)
    ka[...] = jnp.where(low_all, k_low, fk)
    kb[...] = jnp.where(low_all, fk, k_low)
    va[...] = jnp.where(low_all, v_low, one)
    vb[...] = jnp.where(low_all, one, v_low)
    lane = lax.broadcasted_iota(jnp.int32, (block, PAIR), 1)
    low = lane < 64
    spot = lane % 64

    def step(i, carry):
        at = pl.ds(pl.multiple_of(i * block, block), block)
        qb_ = qr_ref[at, :]
        fq = fq_ref[at, :]
        sa = mm(jnp.where(low, qb_, fq), ka[...], NT)
        sb = mm(jnp.where(low, fq, qb_), kb[...], NT)
        ma = jnp.max(sa, axis=1, keepdims=True)
        mb = jnp.max(sb, axis=1, keepdims=True)
        pa = jnp.exp(sa - ma).astype(BF)
        pb = jnp.exp(sb - mb).astype(BF)
        oa = mm(pa, va[...])
        ob = mm(pb, vb[...])
        o = jnp.where(low, oa / pltpu.roll(oa, 64, 1), ob / pltpu.roll(ob, 64, 1))
        o_ref[at, :] = o.astype(o_ref.dtype)
        neg = jnp.where(low, -(mb + jnp.log(ob)), -(ma + jnp.log(oa)))
        hi = neg.astype(BF)
        rest = neg - hi.astype(F32)
        mid = rest.astype(BF)
        last = (rest - mid.astype(F32)).astype(BF)
        fo_ref[at, :] = jnp.where(spot == 8, hi, jnp.where(spot == 9, mid, jnp.where(spot == 10, last, fq)))
        return carry

    lax.fori_loop(0, slots // block, step, 0)


def attention_forward(mixed, cos, sin, fq, fk, first, count, block=256):
    slots, width = mixed.shape
    pairs = width // 3 // PAIR
    blk = lambda off: pl.BlockSpec((slots, PAIR), lambda p: (0, off + p))
    fixed = pl.BlockSpec((slots, PAIR), lambda p: (0, 0))
    out = pl.BlockSpec((slots, PAIR), lambda p: (0, p))
    w = count * PAIR
    elements = 2 * count * slots * slots
    bf = jax.ShapeDtypeStruct((slots, w), BF)
    return pl.pallas_call(
        functools.partial(attention_forward_kernel, block),
        grid=(count,),
        in_specs=[blk(first), blk(pairs + first), blk(2 * pairs + first), fixed, fixed, fixed, fixed],
        out_specs=[out] * 5,
        out_shape=[bf, bf, bf, bf, bf],
        scratch_shapes=[pltpu.VMEM((slots, PAIR), BF)] * 4,
        cost_estimate=pl.CostEstimate(flops=elements * 1000, bytes_accessed=8 * slots * w * 3, transcendentals=elements),
        compiler_params=pltpu.CompilerParams(vmem_limit_bytes=48 * 2**20),
    )(mixed, mixed, mixed, cos, sin, fq, fk)


def attention_backward_kernel(block, qr_ref, kr_ref, vr_ref, fo_ref, fk_ref, do_ref, o_ref, cos_ref, sin_ref,
                              g_ref, ka, kb, va, vb, kt, dka, dkb, dva, dvb):
    slots = qr_ref.shape[0]
    lane_all = lax.broadcasted_iota(jnp.int32, (slots, PAIR), 1)
    low_all = lane_all < 64
    fk = fk_ref[...]
    k_low = kr_ref[...]
    v_low = vr_ref[...]
    one = jnp.where(lane_all % 64 < 2, 1.0, 0.0).astype(BF)
    ka[...] = jnp.where(low_all, k_low, fk)
    kb[...] = jnp.where(low_all, fk, k_low)
    va[...] = jnp.where(low_all, v_low, one)
    vb[...] = jnp.where(low_all, one, v_low)
    kt[...] = k_low.T
    dka[...] = jnp.zeros_like(dka)
    dkb[...] = jnp.zeros_like(dkb)
    dva[...] = jnp.zeros_like(dva)
    dvb[...] = jnp.zeros_like(dvb)
    lane = lax.broadcasted_iota(jnp.int32, (block, PAIR), 1)
    low = lane < 64
    spot = lane % 64
    top = lax.broadcasted_iota(jnp.int32, (PAIR, block), 0) < 64

    def step(i, carry):
        at = pl.ds(pl.multiple_of(i * block, block), block)
        q = qr_ref[at, :]
        fq = fo_ref[at, :]
        do = do_ref[at, :]
        both = do.astype(F32) * o_ref[at, :].astype(F32)
        da = jnp.sum(jnp.where(low, both, 0.0), axis=1, keepdims=True)
        db = jnp.sum(jnp.where(low, 0.0, both), axis=1, keepdims=True)
        neg = jnp.where(low, -db, -da)
        hi = neg.astype(BF)
        rest = (neg - hi.astype(F32)).astype(BF)
        fd = jnp.where(spot == 0, hi, jnp.where(spot == 1, rest, jnp.zeros_like(hi)))
        sa = mm(ka[...], jnp.where(low, q, fq), NT)
        sb = mm(kb[...], jnp.where(low, fq, q), NT)
        ea = mm(va[...], jnp.where(low, do, fd), NT)
        eb = mm(vb[...], jnp.where(low, fd, do), NT)
        pa = jnp.exp(sa)
        pb = jnp.exp(sb)
        dsa = (pa * ea).astype(BF)
        dsb = (pb * eb).astype(BF)
        dva[...] += mm(pa.astype(BF), do)
        dvb[...] += mm(pb.astype(BF), do)
        dka[...] += mm(dsa, q)
        dkb[...] += mm(dsb, q)
        dqt = jnp.where(top, mm(kt[...], dsa), mm(kt[...], dsb))
        dq = dqt.T * 0.125
        g_ref[0, at, :] = (dq * cos_ref[at, :] - swap_halves(dq) * sin_ref[at, :]).astype(BF)
        return carry

    lax.fori_loop(0, slots // block, step, 0)
    dk = jnp.where(low_all, dka[...], dkb[...])
    g_ref[1] = (dk * cos_ref[...] - swap_halves(dk) * sin_ref[...]).astype(BF)
    g_ref[2] = jnp.where(low_all, dva[...], dvb[...]).astype(BF)


def attention_backward(qr, kr, vr, fo, fk, do, o, cos, sin, count, block=256):
    slots, width = qr.shape
    mine = pl.BlockSpec((slots, PAIR), lambda p: (0, p))
    fixed = pl.BlockSpec((slots, PAIR), lambda p: (0, 0))
    w = count * PAIR
    return pl.pallas_call(
        functools.partial(attention_backward_kernel, block),
        grid=(count,),
        in_specs=[mine, mine, mine, mine, fixed, mine, mine, fixed, fixed],
        out_specs=pl.BlockSpec((3, slots, PAIR), lambda p: (0, 0, p)),
        out_shape=jax.ShapeDtypeStruct((3, slots, w), BF),
        scratch_shapes=[pltpu.VMEM((slots, PAIR), BF)] * 4 + [pltpu.VMEM((PAIR, slots), BF)]
        + [pltpu.VMEM((slots, PAIR), F32)] * 4,
        cost_estimate=pl.CostEstimate(
            flops=4 * count * slots * slots * 1000, bytes_accessed=16 * slots * w, transcendentals=2 * count * slots * slots
        ),
        compiler_params=pltpu.CompilerParams(vmem_limit_bytes=48 * 2**20),
    )(qr, kr, vr, fo, fk, do, o, cos, sin)


def attention_tables(segment, position, valid_slot):
    inverse = jnp.exp(jnp.arange(32, dtype=F32) * (-math.log(10000.0) / 32))
    angles = position.astype(F32)[:, None] * inverse[None, :]
    c, s = jnp.cos(angles), jnp.sin(angles)
    cos = jnp.concatenate([c, c, c, c], axis=1)
    sin = jnp.concatenate([-s, s, -s, s], axis=1)
    spot = jnp.arange(PAIR) % 64
    same = segment[:, None] == spot[None, :]
    fq = same.astype(BF)
    fk = jnp.where((spot < 8)[None, :], jnp.where(same & valid_slot[:, None], 0.0, -1e30),
                   jnp.where((spot < 11)[None, :], 1.0, 0.0)).astype(BF)
    return cos, sin, fq, fk


CHIPS = 16
ALONG_X, ALONG_Y, ALONG_Z = (1, 0, 0), (0, 1, 0), (0, 0, 1)
ROUNDS = (
    (((0, 0, 0), ALONG_X), ((0, 0, 0), ALONG_Y), ((0, 0, 0), ALONG_Z)),
    (((0, 1, 0), ALONG_X), ((0, 0, 1), ALONG_Y), ((0, 0, 1), ALONG_Z)),
    (((0, 1, 1), ALONG_X), ((0, 0, 2), ALONG_Y), ((0, 0, 2), ALONG_Z)),
    (((0, 0, 1), ALONG_X), ((0, 0, 3), ALONG_Y), ((1, 1, 1), ALONG_Z)),
    (((0, 0, 3), ALONG_X), ((1, 1, 2), ALONG_Y), ((1, 1, 2), ALONG_Z)),
)
OFFSETS = tuple((a, b, c) for c in range(4) for b in range(2) for a in range(2))


def moved(chip, step, sign=1):
    return ((chip & 1) ^ step[0]) + 2 * (((chip >> 1) & 1) ^ step[1]) + 4 * (((chip >> 2) + sign * step[2]) % 4)


def added(offset, step):
    return (offset[0] ^ step[0], offset[1] ^ step[1], (offset[2] + step[2]) % 4)


ORIGIN = np.array([[moved(chip, offset, -1) for offset in OFFSETS] for chip in range(CHIPS)], np.int32)


def pass_on(values, step, sign=1):
    return lax.ppermute(values, "fsdp", [(chip, moved(chip, step, sign)) for chip in range(CHIPS)])


def swap_core(values):
    return lax.ppermute(values, "rep", [(0, 1), (1, 0)])


def gather_units(unit):
    held = {OFFSETS[0]: unit}
    for round_steps in ROUNDS:
        arrived = [(added(offset, step), pass_on(held[offset], step)) for offset, step in round_steps]
        held.update(arrived)
    return [held[offset] for offset in OFFSETS]


def scatter_units(units, origins):
    sums = {
        offset: lax.dynamic_index_in_dim(units, origins[place], 0, keepdims=False).astype(F32)
        for place, offset in enumerate(OFFSETS)
    }
    for round_steps in reversed(ROUNDS):
        arrived = [
            (offset, pass_on(sums[added(offset, step)].astype(BF), step, -1)) for offset, step in round_steps
        ]
        for offset, values in arrived:
            sums[offset] = sums[offset] + values.astype(F32)
    return sums[OFFSETS[0]]


def sum_small(values):
    for step in (ALONG_X, ALONG_Y, (0, 0, 2)):
        values = values + pass_on(values, step)
    return values + lax.ppermute(values, "fsdp", [(chip, chip ^ 4) for chip in range(CHIPS)])


def place_kernel(plan, count, *refs):
    order_ref, core_ref = refs[:2]
    units = refs[2 : 2 + 2 * CHIPS]
    outs = refs[2 + 2 * CHIPS : -1]
    sems = refs[-1]
    copies = []
    for half in range(2):
        side = core_ref[0] if half == 0 else 1 - core_ref[0]
        for place in range(CHIPS):
            origin = order_ref[place]
            for out, rows, column, width, by_origin, by_side, row, column_side, both in plan:
                if half == 1 and not both:
                    continue
                to_row = pl.multiple_of(origin * by_origin + side * by_side + row, 16)
                to_column = pl.multiple_of(side * column_side, 128) if column_side else 0
                copies.append(
                    pltpu.make_async_copy(
                        units[half * CHIPS + place].at[pl.ds(0, rows), pl.ds(column, width)],
                        outs[out].at[pl.ds(to_row, rows), pl.ds(to_column, width)],
                        sems.at[len(copies)],
                    )
                )
    assert len(copies) == count
    for copy in copies:
        copy.start()
    for copy in copies:
        copy.wait()


def place_units(own, other, order, core, plan, shapes):
    count = sum((2 if piece[-1] else 1) * CHIPS for piece in plan)
    anywhere = pl.BlockSpec(memory_space=pl.ANY)
    scalar = pl.BlockSpec(memory_space=pltpu.SMEM)
    return pl.pallas_call(
        functools.partial(place_kernel, plan, count),
        in_specs=[scalar, scalar] + [anywhere] * (2 * CHIPS),
        out_specs=[anywhere] * len(shapes),
        out_shape=[jax.ShapeDtypeStruct(shape, BF) for shape in shapes],
        scratch_shapes=[pltpu.SemaphoreType.DMA((count,))],
    )(order, core, *own, *other)


SMALL = 128
PLAN_FIRST = (
    (0, 48, 0, 1152, 48, 0, 0, 1152, True),
    (1, 48, 1152, 128, 288, 144, 0, 0, True),
    (1, 48, 1280, 128, 288, 144, 48, 0, True),
    (1, 48, 1408, 128, 288, 144, 96, 0, True),
    (2, 16, 1536, 128, 16, 0, 0, 0, False),
)
PLAN_SECOND = (
    (0, 48, 0, 384, 48, 0, 0, 384, True),
    (1, 48, 384, 1536, 48, 0, 0, 1536, True),
    (2, 48, 1920, 768, 192, 96, 0, 0, True),
    (2, 48, 2688, 768, 192, 96, 48, 0, True),
)


def side_columns(matrix, core, width):
    return lax.dynamic_slice_in_dim(matrix, core * width, width, axis=1)


def side_rows(blocks, core):
    return lax.dynamic_index_in_dim(blocks, core, 1, keepdims=False)


def pack_vectors(rows):
    count = rows.shape[0]
    padded = jnp.pad(rows, ((0, 0), (0, 640 - rows.shape[1]))).reshape(count, 5, 128)
    return jnp.pad(padded, ((0, 0), (0, 43), (0, 0)))


def pack_first(qkv, mod_turned, small, core):
    count = small.shape[0]
    mod_blocks = side_rows(mod_turned.reshape(count, 2, 3, 48, 128), core)
    return jnp.concatenate(
        [
            side_columns(qkv, core, 1152).reshape(count, 48, 1152),
            mod_blocks.transpose(0, 2, 1, 3).reshape(count, 48, 384),
            pack_vectors(small),
        ],
        axis=2,
    )


def pack_second(out, up, down, core):
    count = out.shape[0] // 48
    down_blocks = side_rows(down.reshape(count, 2, 2, 48, D), core)
    return jnp.concatenate(
        [
            side_columns(out, core, 384).reshape(count, 48, 384),
            side_columns(up, core, 1536).reshape(count, 48, 1536),
            down_blocks.transpose(0, 2, 1, 3).reshape(count, 48, 2 * D),
        ],
        axis=2,
    )


def gather_first(qkv, mod, vectors, chip, core):
    if lax.axis_size("fsdp") != CHIPS:
        return (
            lax.all_gather(qkv, "fsdp", axis=0, tiled=True),
            lax.all_gather(mod, "fsdp", axis=1, tiled=True).T,
            lax.all_gather(vectors, "fsdp", axis=0, tiled=True),
        )
    unit = pack_first(qkv, mod.T, vectors[None], core)[0]
    own = gather_units(unit)
    other = [swap_core(one) for one in own]
    qkv_all, mod_all, small = place_units(
        own, other, jnp.asarray(ORIGIN)[chip], core[None], PLAN_FIRST, ((D, 3 * D), (6 * D, COND), (256, 128))
    )
    return (qkv_all, mod_all, small.reshape(CHIPS, 2048)[:, :624].reshape(-1))


def gather_second(out, up, down, chip, core):
    if lax.axis_size("fsdp") != CHIPS:
        return tuple(lax.all_gather(part, "fsdp", axis=0, tiled=True) for part in (out, up, down))
    own = gather_units(pack_second(out, up, down, core)[0])
    other = [swap_core(one) for one in own]
    return place_units(
        own, other, jnp.asarray(ORIGIN)[chip], core[None], PLAN_SECOND, ((D, D), (D, FF), (FF, D))
    )


def reduce_packed(pack, chip, core):
    arrived = swap_core(pack(1 - core).astype(BF))
    units = (pack(core).astype(F32) + arrived.astype(F32)).astype(BF)
    mine = scatter_units(units, jnp.asarray(ORIGIN)[chip]).astype(BF)
    other = swap_core(mine)
    first = jnp.where(core == 0, mine, other).astype(F32)
    second = jnp.where(core == 0, other, mine).astype(F32)
    return (first, second)


def reduce_plain(grad, axis):
    part = lax.psum_scatter(grad.astype(F32), "fsdp", scatter_dimension=axis, tiled=True)
    return lax.psum(part.astype(BF), "rep").astype(F32)


def reduce_first(qkv, mod_turned, vectors, chip, core):
    if lax.axis_size("fsdp") != CHIPS:
        return (reduce_plain(qkv, 0), reduce_plain(mod_turned.T, 1), reduce_plain(vectors, 0))
    small = vectors.reshape(CHIPS, -1)
    first, second = reduce_packed(lambda side: pack_first(qkv, mod_turned, small.astype(BF), side), chip, core)
    turned = jnp.concatenate(
        [half[:, 1152 + 128 * part : 1280 + 128 * part] for half in (first, second) for part in range(3)], axis=0
    )
    return (
        jnp.concatenate([first[:, :1152], second[:, :1152]], axis=1),
        turned.T,
        first[:5, 1536:].reshape(-1)[:624],
    )


def reduce_second(out, up, down, chip, core):
    if lax.axis_size("fsdp") != CHIPS:
        return (reduce_plain(out, 0), reduce_plain(up, 0), reduce_plain(down, 0))
    first, second = reduce_packed(lambda side: pack_second(out, up, down, side), chip, core)
    return (
        jnp.concatenate([first[:, :384], second[:, :384]], axis=1),
        jnp.concatenate([first[:, 384:1920], second[:, 384:1920]], axis=1),
        jnp.concatenate([half[:, 1920 + D * part : 2688 + D * part] for half in (first, second) for part in range(2)], axis=0),
    )


def sum_over_chips(values):
    if lax.axis_size("fsdp") != CHIPS:
        return lax.psum(values, "fsdp")
    return sum_small(values)


def linear(left_side, right_side, dims=NN):
    return lax.dot_general(left_side, right_side, dims, preferred_element_type=F32)


def precise(left_side, right_side, dims=NN):
    return lax.dot_general(
        left_side, right_side, dims, precision=lax.Precision.HIGHEST, preferred_element_type=F32
    )


def layout_tables(sizes_row, lengths_row):
    slot_ids = jnp.arange(SLOTS, dtype=jnp.int32)
    seg_ends = jnp.cumsum(sizes_row)
    starts = seg_ends - sizes_row
    segment = jnp.sum((slot_ids[:, None] >= seg_ends[None, :]).astype(jnp.int32), axis=1)
    member = segment[:, None] == jnp.arange(NSEG, dtype=jnp.int32)[None, :]
    offset = jnp.sum(jnp.where(member, starts[None, :], 0), axis=1)
    length_of = jnp.sum(jnp.where(member, lengths_row[None, :], 0), axis=1)
    position = slot_ids - offset
    return (segment, member, position, position < length_of)


def condition(steps_row):
    half_cond = COND // 2
    frequency = jnp.exp(jnp.arange(half_cond, dtype=F32) * (-math.log(10000.0) / half_cond))
    angles = steps_row.astype(F32)[:, None] * frequency[None, :]
    return jax.nn.silu(jnp.concatenate([jnp.cos(angles), jnp.sin(angles)], axis=1))


def normalize(values):
    average = jnp.mean(values, axis=-1, keepdims=True)
    centered = values - average
    root = lax.rsqrt(jnp.mean(centered * centered, axis=-1, keepdims=True) + 1e-05)
    return (centered * root, root)


def normalize_back(grad, normal, root, gain):
    scaled = grad * gain
    inner = jnp.mean(scaled * normal, axis=-1, keepdims=True)
    return root * (scaled - jnp.mean(scaled, axis=-1, keepdims=True) - normal * inner)


def gelu_slope(values):
    factor = math.sqrt(2.0 / math.pi)
    square = values * values
    bent = jnp.tanh(factor * values * (1.0 + 0.044715 * square))
    return 0.5 * (1.0 + bent) + 0.5 * values * (1.0 - bent * bent) * factor * (1.0 + 3 * 0.044715 * square)


def tiled(values):
    return values.reshape(BLOCKS, TILE, values.shape[-1])


def flat(values):
    return values.reshape(SLOTS, values.shape[-1])


def adam_direction(weight, first_old, second_old, gradient, decay_rate):
    first_new = BETA_ONE * first_old + (1.0 - BETA_ONE) * gradient
    second_new = BETA_TWO * second_old + (1.0 - BETA_TWO) * gradient * gradient
    direction = (
        first_new
        / (1.0 - BETA_ONE**STEP)
        / (jnp.sqrt(second_new / (1.0 - BETA_TWO**STEP)) + EPSILON)
        + decay_rate * weight
    )
    return (first_new, second_new, direction)


GROUPS = 3


def on_device(
    inputs, cotangent, seg_sizes, seq_lengths, timesteps, absorbed,
    qkv_weight, out_weight, up_weight, down_weight, mod_weight,
    qkv_first, out_first, up_first, down_first, mod_first,
    qkv_second, out_second, up_second, down_second, mod_second,
    vectors, vectors_first, vectors_second,
):
    chip = lax.axis_index("fsdp")
    core = lax.axis_index("rep")
    matrices = (qkv_weight, out_weight, up_weight, down_weight, mod_weight)
    weight_squares = jnp.stack([jnp.sum(matrix * matrix) for matrix in matrices])
    low = [matrix.astype(BF) for matrix in matrices]
    qkv_low, mod_turned, vector_low = gather_first(low[0], low[4], vectors.astype(BF), chip, core)
    out_low, up_low, down_low = gather_second(low[1], low[2], low[3], chip, core)

    vector_all = vector_low.astype(F32)
    gain_one, gain_two = vector_all[:D], vector_all[D : 2 * D]
    bias_up = vector_all[2 * D : 2 * D + FF]
    bias_down = vector_all[2 * D + FF : 3 * D + FF]
    bias_mod = vector_all[3 * D + FF :]

    segment, member, position, valid_slot = layout_tables(seg_sizes[0], seq_lengths[0])
    member_tile = member.reshape(BLOCKS, TILE, NSEG)[:, 0].astype(F32)
    condition_low = condition(timesteps[0]).astype(BF)
    modulation = linear(condition_low, mod_turned, NT) + bias_mod
    per_tile = precise(member_tile, modulation)[:, None, :]
    shift_one, scale_one, gate_one, shift_two, scale_two, gate_two = jnp.split(per_tile, 6, axis=2)
    cos, sin, feature_query, feature_key = attention_tables(segment, position, valid_slot)

    wide = tiled(inputs[0].astype(F32))
    normal_one, root_one = normalize(wide)
    first_low = flat(normal_one * gain_one * (1.0 + scale_one) + shift_one).astype(BF)
    mixed = linear(first_low, qkv_low)
    per_call = HEADS // 2 // GROUPS
    forward = [
        attention_forward(mixed, cos, sin, feature_query, feature_key, number * per_call, per_call)
        for number in range(GROUPS)
    ]
    attended_low = jnp.concatenate([part[0] for part in forward], axis=1)
    branch = tiled(linear(attended_low, out_low))
    middle = wide + gate_one * branch
    normal_two, root_two = normalize(middle)
    second_low = flat(normal_two * gain_two * (1.0 + scale_two) + shift_two).astype(BF)
    up_values = linear(second_low, up_low) + bias_up
    hidden_low = jax.nn.gelu(up_values, approximate=True).astype(BF)
    feed_out = tiled(linear(hidden_low, down_low) + bias_down)
    out_hidden = flat(middle + gate_two * feed_out).astype(BF)

    weight_mask = (absorbed[0] * valid_slot.astype(jnp.int32)).astype(F32)
    grad_out = tiled(cotangent[0].astype(F32) * weight_mask[:, None])
    grad_mlp = flat(grad_out * gate_two).astype(BF)
    grad_gate_two = jnp.sum(grad_out * feed_out, axis=1)
    grad_down = linear(hidden_low, grad_mlp, TN).astype(BF)
    grad_up = (linear(grad_mlp, down_low, NT) * gelu_slope(up_values)).astype(BF)
    grad_up_weight = linear(second_low, grad_up, TN).astype(BF)
    grad_second = tiled(linear(grad_up, up_low, NT))
    sum_two = jnp.sum(grad_second, axis=1)
    inner_two = jnp.sum(grad_second * normal_two, axis=1)
    grad_middle = grad_out + normalize_back(grad_second, normal_two, root_two, gain_two * (1.0 + scale_two))
    grad_gate_one = jnp.sum(grad_middle * branch, axis=1)
    grad_branch = flat(grad_middle * gate_one).astype(BF)
    grad_attn_out = linear(attended_low, grad_branch, TN).astype(BF)
    grad_attended = linear(grad_branch, out_low, NT).astype(BF)
    later = reduce_second(grad_attn_out, grad_up_weight, grad_down, chip, core)

    backward = []
    for number, (part, query, key, value, feature) in enumerate(forward):
        width = per_call * PAIR
        grad_part = grad_attended[:, number * width : (number + 1) * width]
        backward.append(attention_backward(query, key, value, feature, feature_key, grad_part, part, cos, sin, per_call))
    grad_mixed = jnp.concatenate([part[kind] for kind in range(3) for part in backward], axis=1)
    grad_qkv = linear(first_low, grad_mixed, TN).astype(BF)
    grad_first = tiled(linear(grad_mixed, qkv_low, NT))
    sum_one = jnp.sum(grad_first, axis=1)
    inner_one = jnp.sum(grad_first * normal_one, axis=1)
    grad_in = flat(grad_middle + normalize_back(grad_first, normal_one, root_one, gain_one * (1.0 + scale_one)))

    tile_grads = jnp.concatenate(
        [sum_one, inner_one * gain_one, grad_gate_one, sum_two, inner_two * gain_two, grad_gate_two], axis=1
    )
    grad_modulation = precise(member_tile, tile_grads, TN)
    grad_mod = precise(grad_modulation, condition_low.astype(F32), TN).astype(BF)
    grad_vectors = jnp.concatenate(
        [
            jnp.sum(inner_one * (1.0 + scale_one[:, 0]), axis=0),
            jnp.sum(inner_two * (1.0 + scale_two[:, 0]), axis=0),
            jnp.sum(grad_up.astype(F32), axis=0),
            jnp.sum(grad_mlp.astype(F32), axis=0),
            jnp.sum(grad_modulation, axis=0),
        ]
    )
    sooner = reduce_first(grad_qkv, grad_mod, grad_vectors, chip, core)

    grads = (sooner[0], later[0], later[1], later[2], sooner[1])
    firsts = (qkv_first, out_first, up_first, down_first, mod_first)
    seconds = (qkv_second, out_second, up_second, down_second, mod_second)
    results = [
        adam_direction(matrices[number], firsts[number], seconds[number], grads[number], DECAY_RATE)
        for number in range(5)
    ]
    update_squares = jnp.stack([jnp.sum(record[2] * record[2]) for record in results])
    norm_roots = jnp.sqrt(sum_over_chips(jnp.stack([weight_squares, update_squares])))
    trust = norm_roots[0] / (norm_roots[1] + EPSILON)
    renewed = [
        matrices[number] - MATRIX_RATE * trust[number] * results[number][2] for number in range(5)
    ]
    vector_record = adam_direction(vectors, vectors_first, vectors_second, sooner[2], 0.0)
    return (
        out_hidden[None],
        grad_in[None],
        *renewed,
        *[record[0] for record in results],
        *[record[1] for record in results],
        vectors - VECTOR_RATE * vector_record[2],
        vector_record[0],
        vector_record[1],
        norm_roots,
    )


def solution(mesh):
    rows = P(("rep", "fsdp"))
    matrix, turned, vector = P("fsdp", None), P(None, "fsdp"), P("fsdp")
    five = (matrix, matrix, matrix, matrix, turned)
    return jax.shard_map(
        on_device,
        mesh=mesh,
        in_specs=(rows,) * 6 + five * 3 + (vector,) * 3,
        out_specs=(rows, rows) + five * 3 + (vector,) * 3 + (P(),),
        check_vma=False,
    )
```

time: 1470 us -> 987 us (0.67)
  waiting for transfers between devices: 733 us -> 79 us
  Pallas kernels: 0 us -> 550 us
  matrix products: 397 us -> 97.5 us
  blocking collectives: 160 us -> 0 us
  starting transfers between devices: 0.63 us -> 88.7 us
  other arithmetic: 106 us -> 64.4 us
  local copies, waits for them, and re-layouts: 41.9 us -> 60.5 us
    reduce_scatter x5 -> x0, waiting for transfers between devices: 595 us -> none  [the longest x1 175 us: on_device(): lax.psum_scatter(summed_grads[2], 'fsdp', scatter_dimension=0, tiled=True)]
    pallas_call x0 -> x8, Pallas kernels: none -> 550 us  [the longest x2 473 us: place_units(): pl.pallas_call(functools.partial(place_kernel, plan, count), in_specs=[sc...]
    dot_general x27 -> x16, matrix products: 383 us -> 97.5 us  [the longest x13 94.8 us: linear(): lax.dot_general(left_side, right_side, dims, preferred_element_type=F32)]
    all_gather x5 -> x0, waiting for transfers between devices: 117 us -> none  [the longest x1 69.1 us: on_device(): lax.all_gather(sent[3], 'fsdp', axis=0, tiled=True)]
    ppermute x0 -> x100, starting transfers between devices: none -> 88.7 us  [the longest x63 80.1 us: pass_on(): lax.ppermute(values, 'fsdp', [(chip, moved(chip, step, sign)) for chip in...]
    psum x2 -> x0, blocking collectives: 80.8 us -> none  [the longest x1 78.4 us: on_device(): summed = lax.psum(squares, 'fsdp')]
    ppermute x0 -> x100, waiting for transfers between devices: none -> 79 us  [the longest x63 77.2 us: pass_on(): lax.ppermute(values, 'fsdp', [(chip, moved(chip, step, sign)) for chip in...]
    unnamed x1 -> x0, blocking collectives: 78.8 us -> none
  transfers between devices with their start and end apart: 11 -> 100, of which waited for: 8 -> 25; matrix products, arithmetic and copies ran while one was open for 22% -> 7% of each run, Pallas kernels for 0% -> 18%
where the time goes in v1:
time: 987 us; the launch traced here: 977 us
  Pallas kernels  550 us (56%)
  matrix products  97.5 us (10%)
  starting transfers between devices  88.7 us (9%)
  waiting for transfers between devices  79 us (8%)
  other arithmetic  64.4 us (7%)
  local copies, waits for them, and re-layouts  60.5 us (6%)
  between operations  37.5 us (4%)
    pallas_call x2, Pallas kernels, place_units(): pl.pallas_call(functools.partial(place_kernel, plan, count), in_specs=[sc...  473 us
    dot_general x13, matrix products, linear(): lax.dot_general(left_side, right_side, dims, preferred_element_type=F32)  94.8 us
    ppermute x63, starting transfers between devices, pass_on(): lax.ppermute(values, 'fsdp', [(chip, moved(chip, step, sign)) for chip in...  80.1 us
    ppermute x63, waiting for transfers between devices, pass_on(): lax.ppermute(values, 'fsdp', [(chip, moved(chip, step, sign)) for chip in...  77.2 us
    pallas_call x3, Pallas kernels, attention_backward(): pl.pallas_call(functools.partial(attention_backward_kernel, block), grid=...  45.6 us
    pallas_call x3, Pallas kernels, attention_forward(): pl.pallas_call(functools.partial(attention_forward_kernel, block), grid=(...  31.4 us
    unnamed x359, local copies, waits for them, and re-layouts  29.7 us
  transfers between devices with their start and end apart: 100, of which 25 were waited for; matrix products, arithmetic and copies ran while one was open for 7% of the time, Pallas kernels for 18%

profile of v1, /device:TPU:0, one launch (start us, length us, event | category | flops | bytes accessed | tf_op | source)
XLA Modules:
  0.0 977.2 jit_solution(635789245936643699)
XLA Ops:
  33.8 5.8 collective-permute-done.6.refs_9_
  44.0 5.3 collective-permute-done.8.refs_13_
  66.9 148.0 %shard_map.400 = (bf16[768,2304]{1,0:T(8,128)(2,1)}, bf16[4608,128]{1,0:T(8,128)(2,1)}, bf16[256,128]{1,0:T(8,128)(2,1)}) custom-call(s32[16]{0:T(128)} %get-tuple-element.165.refs_0_, s32[1]{0:T(128)} %bitcast.7.refs_1_, bf16[48,1664]{1,0:T(8,128)(2,1)} %copy-done.65, bf16[48,1664]{1,0:T(8,128)(2,1)} %copy-done.105, bf16[48,1664]{1,0:T(8,128)(2,1)} %copy-done.104, ...), custom_call_target="tpu_custom_call" | custom-call | tf_op jit(solution)/shard_map/pallas_call | solution.py:299
  225.2 6.2 fusion.135.q_ref.k_ref.v_ref
  234.8 4.8 collective-permute-done.33.refs_5_
  240.4 10.5 %shard_map.402 = (bf16[1024,256]{1,0:T(8,128)(2,1)S(1)}, bf16[1024,256]{1,0:T(8,128)(2,1)S(1)}, bf16[1024,256]{1,0:T(8,128)(2,1)S(1)}, bf16[1024,256]{1,0:T(8,128)(2,1)S(1)}, bf16[1024,256]{1,0:T(8,128)(2,1)S(1)}) custom-call(f32[1024,2304]{1,0:T(8,128)} %fusion.135.q_ref.k_ref.v_ref, f32[1024,2304]{1,0:T(8,128)} %fusion.135.q_ref.k_ref.v_ref, ...), custom_call_target="tpu_custom_call" | custom-call | flops 4194304000 | bytes 6291456 | tf_op jit(solution)/shard_map/pallas_call | solution.py:103
  254.8 10.4 %shard_map.401 = (bf16[1024,256]{1,0:T(8,128)(2,1)S(1)}, bf16[1024,256]{1,0:T(8,128)(2,1)S(1)}, bf16[1024,256]{1,0:T(8,128)(2,1)S(1)}, bf16[1024,256]{1,0:T(8,128)(2,1)S(1)}, bf16[1024,256]{1,0:T(8,128)(2,1)S(1)}) custom-call(f32[1024,2304]{1,0:T(8,128)} %fusion.135.q_ref.k_ref.v_ref, f32[1024,2304]{1,0:T(8,128)} %fusion.135.q_ref.k_ref.v_ref, ...), custom_call_target="tpu_custom_call" | custom-call | flops 4194304000 | bytes 6291456 | tf_op jit(solution)/shard_map/pallas_call | solution.py:103
  267.8 10.5 %shard_map.403 = (bf16[1024,256]{1,0:T(8,128)(2,1)S(1)}, bf16[1024,256]{1,0:T(8,128)(2,1)S(1)}, bf16[1024,256]{1,0:T(8,128)(2,1)S(1)}, bf16[1024,256]{1,0:T(8,128)(2,1)S(1)}, bf16[1024,256]{1,0:T(8,128)(2,1)S(1)}) custom-call(f32[1024,2304]{1,0:T(8,128)} %fusion.135.q_ref.k_ref.v_ref, f32[1024,2304]{1,0:T(8,128)} %fusion.135.q_ref.k_ref.v_ref, ...), custom_call_target="tpu_custom_call" | custom-call | flops 4194304000 | bytes 6291456 | tf_op jit(solution)/shard_map/pallas_call | solution.py:103
  285.6 324.6 %shard_map.404 = (bf16[768,768]{1,0:T(8,128)(2,1)}, bf16[768,3072]{1,0:T(8,128)(2,1)}, bf16[3072,768]{1,0:T(8,128)(2,1)}) custom-call(s32[16]{0:T(128)} %get-tuple-element.165.refs_0_, s32[1]{0:T(128)} %bitcast.7.refs_1_, bf16[48,3456]{1,0:T(8,128)(2,1)} %copy-done.59, bf16[48,3456]{1,0:T(8,128)(2,1)} %collective-permute-done.31.refs_3_, ...), custom_call_target="tpu_custom_call" | custom-call | tf_op jit(solution)/shard_map/pallas_call | solution.py:299
  610.1 4.9 bitcast_multiply_fusion.3
  618.5 7.8 fusion.136
  626.4 12.3 %convolution_convert_fusion.1 = bf16[3072,768]{1,0:T(8,128)(2,1)} fusion(bf16[1024,768]{1,0:T(8,128)(2,1)S(1)} %copy-done.58, f32[1024,3072]{1,0:T(8,128)} %fusion.136, f32[3072]{0:T(1024)S(1)} %slice.282), kind=kOutput, calls=%fused_computation.27 | convolution fusion | flops 4865654784 | bytes 18886656 | tf_op jit(solution)/shard_map/dot_general | solution.py:438
  638.7 14.2 %fusion.133 = (bf16[3072]{0:T(1024)(128)(2,1)}, bf16[1024,3072]{1,0:T(8,128)(2,1)S(1)}) fusion(f32[1024,3072]{1,0:T(8,128)} %fusion.136, f32[3072]{0:T(1024)S(1)} %slice.282, bf16[1024,768]{1,0:T(8,128)(2,1)S(1)} %copy-done.58, bf16[3072,768]{1,0:T(8,128)(2,1)} %get-tuple-element.50), kind=kOutput, calls=%fused_computation.341 | convolution fusion | flops 4894749696 | bytes 25184256 | tf_op jit(solution)/shard_map/dot_general | solution.py:438
  652.9 6.8 convolution_convert_fusion.2
  659.7 9.2 fusion.39
  669.0 15.9 %fusion.17 = (bf16[1024,768]{1,0:T(8,128)(2,1)S(1)}, bf16[1024,768]{1,0:T(8,128)(2,1)}, f32[1024,768]{1,0:T(8,128)}) fusion(bf16[1,1024,768]{2,1,0:T(8,128)(2,1)S(1)} %copy-done.32, f32[1024,768]{1,0:T(8,128)S(1)} %get-tuple-element.207, f32[1024]{0:T(1024)S(1)} %get-tuple-element.180, f32[1024]{0:T(1024)S(1)} %get-tuple-element.176, ...), kind=kOutput, calls=%fused_computation.34 | convolution fusion | flops 4877451264 | bytes 33139712 | tf_op jit(solution)/shard_map/dot_general | solution.py:438
  689.0 15.1 %shard_map.405 = bf16[3,1024,256]{2,1,0:T(8,128)(2,1)S(1)} custom-call(bf16[1024,256]{1,0:T(8,128)(2,1)S(1)} %copy-done.9, bf16[1024,256]{1,0:T(8,128)(2,1)S(1)} %copy-done.11, bf16[1024,256]{1,0:T(8,128)(2,1)S(1)} %copy-done.13, bf16[1024,256]{1,0:T(8,128)(2,1)S(1)} %copy-done.15, bf16[1024,128]{1,0:T(8,128)(2,1)S(1)} %select_convert_fusion.fk_ref, ...), custom_call_target="tpu_custom_call" | custom-call | flops 8388608000 | bytes 4194304 | tf_op jit(solution)/shard_map/pallas_call | solution.py:178
  705.0 15.1 %shard_map.406 = bf16[3,1024,256]{2,1,0:T(8,128)(2,1)S(1)} custom-call(bf16[1024,256]{1,0:T(8,128)(2,1)S(1)} %copy-done.1, bf16[1024,256]{1,0:T(8,128)(2,1)S(1)} %copy-done.3, bf16[1024,256]{1,0:T(8,128)(2,1)S(1)} %copy-done.5, bf16[1024,256]{1,0:T(8,128)(2,1)S(1)} %copy-done.7, bf16[1024,128]{1,0:T(8,128)(2,1)S(1)} %select_convert_fusion.fk_ref, ...), custom_call_target="tpu_custom_call" | custom-call | flops 8388608000 | bytes 4194304 | tf_op jit(solution)/shard_map/pallas_call | solution.py:178
  721.0 15.5 %shard_map.407 = bf16[3,1024,256]{2,1,0:T(8,128)(2,1)S(1)} custom-call(bf16[1024,256]{1,0:T(8,128)(2,1)S(1)} %copy-done.17, bf16[1024,256]{1,0:T(8,128)(2,1)S(1)} %copy-done.19, bf16[1024,256]{1,0:T(8,128)(2,1)S(1)} %copy-done.21, bf16[1024,256]{1,0:T(8,128)(2,1)S(1)} %copy-done.23, bf16[1024,128]{1,0:T(8,128)(2,1)S(1)} %select_convert_fusion.fk_ref, ...), custom_call_target="tpu_custom_call" | custom-call | flops 8388608000 | bytes 4194304 | tf_op jit(solution)/shard_map/pallas_call | solution.py:178
  742.7 7.8 convolution_convert_fusion.3
  865.4 5.6 fusion.25
  881.9 5.2 collective-permute-done.81
  887.6 6.1 collective-permute-done.90
  898.4 6.8 collective-permute-done.86
  (689 shorter events, 265.4 us)
Async XLA Ops:
  3.6 16.6 %collective-permute-start.3 = (bf16[48,1664]{1,0:T(8,128)(2,1)S(1)}, bf16[48,1664]{1,0:T(8,128)(2,1)S(1)}, u32[]{:S(2)}, u32[]{:S(2)}) collective-permute-start(bf16[48,1664]{1,0:T(8,128)(2,1)S(1)} %fusion.89.refs_2_), channel_id=1, source_target_pairs={{0,4},{1,5},{2,6},{3,7},{4,8},{5,9},{6,10},{7,11},{8,12},{9,13},{1... | collective-permute-start | bytes 479240 | tf_op jit(solution)/shard_map/ppermute | solution.py:231
  8.1 14.1 %collective-permute-start = (bf16[48,1664]{1,0:T(8,128)(2,1)S(1)}, bf16[48,1664]{1,0:T(8,128)(2,1)S(1)}, u32[]{:S(2)}, u32[]{:S(2)}) collective-permute-start(bf16[48,1664]{1,0:T(8,128)(2,1)S(1)} %fusion.89.refs_2_), channel_id=1, source_target_pairs={{0,1},{1,0},{2,3},{3,2},{4,5},{5,4},{6,7},{7,6},{8,9},{9,8},{10,11... | collective-permute-start | bytes 479240 | tf_op jit(solution)/shard_map/ppermute | solution.py:231
  12.9 20.6 %collective-permute-start.34 = (bf16[48,3456]{1,0:T(8,128)(2,1)S(1)}, bf16[48,3456]{1,0:T(8,128)(2,1)S(1)}, u32[]{:S(2)}, u32[]{:S(2)}) collective-permute-start(bf16[48,3456]{1,0:T(8,128)(2,1)S(1)} %maximum_bitcast_fusion.refs_2_), channel_id=1, source_target_pairs={{0,4},{1,5},{2,6},{3,7},{4,8},{5,9},{6,10},{7,11},{8,12},{9,13},{1... | collective-permute-start | bytes 995336 | tf_op jit(solution)/shard_map/ppermute | solution.py:231
  63.3 159.3 %collective-permute-start.32 = (bf16[48,3456]{1,0:T(8,128)(2,1)S(1)}, bf16[48,3456]{1,0:T(8,128)(2,1)}, u32[]{:S(2)}, u32[]{:S(2)}) collective-permute-start(bf16[48,3456]{1,0:T(8,128)(2,1)S(1)} %maximum_bitcast_fusion.refs_2_), channel_id=1, source_target_pairs={{0,2},{1,3},{2,0},{3,1},{4,6},{5,7},{6,4},{7,5},{8,10},{9,11},{10,... | collective-permute-start | bytes 995336 | tf_op jit(solution)/shard_map/ppermute | solution.py:231
  64.3 158.8 %collective-permute-start.31 = (bf16[48,3456]{1,0:T(8,128)(2,1)S(1)}, bf16[48,3456]{1,0:T(8,128)(2,1)}, u32[]{:S(2)}, u32[]{:S(2)}) collective-permute-start(bf16[48,3456]{1,0:T(8,128)(2,1)S(1)} %maximum_bitcast_fusion.refs_2_), channel_id=1, source_target_pairs={{0,1},{1,0},{2,3},{3,2},{4,5},{5,4},{6,7},{7,6},{8,9},{9,8},{10,11... | collective-permute-start | bytes 995336 | tf_op jit(solution)/shard_map/ppermute | solution.py:231
  65.8 157.3 %collective-permute-start.46 = (bf16[48,3456]{1,0:T(8,128)(2,1)S(1)}, bf16[48,3456]{1,0:T(8,128)(2,1)}, u32[]{:S(2)}, u32[]{:S(2)}) collective-permute-start(bf16[48,3456]{1,0:T(8,128)(2,1)S(1)} %maximum_bitcast_fusion.refs_2_), channel_id=1, source_target_pairs={{0,16},{16,0},{1,17},{17,1},{2,18},{18,2},{3,19},{19,3},{4,20},{20... | collective-permute-start | bytes 995336 | tf_op jit(solution)/shard_map/ppermute | solution.py:235
  65.8 158.9 %collective-permute-start.36 = (bf16[48,3456]{1,0:T(8,128)(2,1)}, bf16[48,3456]{1,0:T(8,128)(2,1)}, u32[]{:S(2)}, u32[]{:S(2)}) collective-permute-start(bf16[48,3456]{1,0:T(8,128)(2,1)} %copy-done.74), channel_id=1, source_target_pairs={{0,2},{1,3},{2,0},{3,1},{4,6},{5,7},{6,4},{7,5},{8,10},{9,11},{10,... | collective-permute-start | bytes 995336 | tf_op jit(solution)/shard_map/ppermute | solution.py:231
  66.9 157.9 %collective-permute-start.38 = (bf16[48,3456]{1,0:T(8,128)(2,1)}, bf16[48,3456]{1,0:T(8,128)(2,1)}, u32[]{:S(2)}, u32[]{:S(2)}) collective-permute-start(bf16[48,3456]{1,0:T(8,128)(2,1)} %copy-done.74), channel_id=1, source_target_pairs={{0,4},{1,5},{2,6},{3,7},{4,8},{5,9},{6,10},{7,11},{8,12},{9,13},{1... | collective-permute-start | bytes 995336 | tf_op jit(solution)/shard_map/ppermute | solution.py:231
  223.1 16.4 %collective-permute-start.33 = (bf16[48,3456]{1,0:T(8,128)(2,1)}, bf16[48,3456]{1,0:T(8,128)(2,1)S(1)}, u32[]{:S(2)}, u32[]{:S(2)}) collective-permute-start(bf16[48,3456]{1,0:T(8,128)(2,1)} %collective-permute-done.32.refs_4_), channel_id=1, source_target_pairs={{0,1},{1,0},{2,3},{3,2},{4,5},{5,4},{6,7},{7,6},{8,9},{9,8},{10,11... | collective-permute-start | bytes 995336 | tf_op jit(solution)/shard_map/ppermute | solution.py:231
  224.7 14.9 %collective-permute-start.48 = (bf16[48,3456]{1,0:T(8,128)(2,1)}, bf16[48,3456]{1,0:T(8,128)(2,1)S(1)}, u32[]{:S(2)}, u32[]{:S(2)}) collective-permute-start(bf16[48,3456]{1,0:T(8,128)(2,1)} %collective-permute-done.32.refs_4_), channel_id=1, source_target_pairs={{0,16},{16,0},{1,17},{17,1},{2,18},{18,2},{3,19},{19,3},{4,20},{20... | collective-permute-start | bytes 995336 | tf_op jit(solution)/shard_map/ppermute | solution.py:235
  224.9 15.3 %collective-permute-start.47 = (bf16[48,3456]{1,0:T(8,128)(2,1)}, bf16[48,3456]{1,0:T(8,128)(2,1)S(1)}, u32[]{:S(2)}, u32[]{:S(2)}) collective-permute-start(bf16[48,3456]{1,0:T(8,128)(2,1)} %collective-permute-done.31.refs_3_), channel_id=1, source_target_pairs={{0,16},{16,0},{1,17},{17,1},{2,18},{18,2},{3,19},{19,3},{4,20},{20... | collective-permute-start | bytes 995336 | tf_op jit(solution)/shard_map/ppermute | solution.py:235
  233.2 18.2 %collective-permute-start.42 = (bf16[48,3456]{1,0:T(8,128)(2,1)}, bf16[48,3456]{1,0:T(8,128)(2,1)S(1)}, u32[]{:S(2)}, u32[]{:S(2)}) collective-permute-start(bf16[48,3456]{1,0:T(8,128)(2,1)} %collective-permute-done.38.refs_10_), channel_id=1, source_target_pairs={{0,4},{1,5},{2,6},{3,7},{4,8},{5,9},{6,10},{7,11},{8,12},{9,13},{1... | collective-permute-start | bytes 995336 | tf_op jit(solution)/shard_map/ppermute | solution.py:231
  233.7 17.9 %collective-permute-start.41 = (bf16[48,3456]{1,0:T(8,128)(2,1)}, bf16[48,3456]{1,0:T(8,128)(2,1)S(1)}, u32[]{:S(2)}, u32[]{:S(2)}) collective-permute-start(bf16[48,3456]{1,0:T(8,128)(2,1)} %collective-permute-done.38.refs_10_), channel_id=1, source_target_pairs={{0,2},{1,3},{2,0},{3,1},{4,6},{5,7},{6,4},{7,5},{8,10},{9,11},{10,... | collective-permute-start | bytes 995336 | tf_op jit(solution)/shard_map/ppermute | solution.py:231
  250.9 14.5 %collective-permute-start.51 = (bf16[48,3456]{1,0:T(8,128)(2,1)S(1)}, bf16[48,3456]{1,0:T(8,128)(2,1)S(1)}, u32[]{:S(2)}, u32[]{:S(2)}) collective-permute-start(bf16[48,3456]{1,0:T(8,128)(2,1)S(1)} %collective-permute-done.35.refs_7_), channel_id=1, source_target_pairs={{0,16},{16,0},{1,17},{17,1},{2,18},{18,2},{3,19},{19,3},{4,20},{20... | collective-permute-start | bytes 995336 | tf_op jit(solution)/shard_map/ppermute | solution.py:235
  251.4 14.1 %collective-permute-start.49 = (bf16[48,3456]{1,0:T(8,128)(2,1)S(1)}, bf16[48,3456]{1,0:T(8,128)(2,1)S(1)}, u32[]{:S(2)}, u32[]{:S(2)}) collective-permute-start(bf16[48,3456]{1,0:T(8,128)(2,1)S(1)} %collective-permute-done.33.refs_5_), channel_id=1, source_target_pairs={{0,16},{16,0},{1,17},{17,1},{2,18},{18,2},{3,19},{19,3},{4,20},{20... | collective-permute-start | bytes 995336 | tf_op jit(solution)/shard_map/ppermute | solution.py:235
  251.6 14.6 %collective-permute-start.43 = (bf16[48,3456]{1,0:T(8,128)(2,1)S(1)}, bf16[48,3456]{1,0:T(8,128)(2,1)S(1)}, u32[]{:S(2)}, u32[]{:S(2)}) collective-permute-start(bf16[48,3456]{1,0:T(8,128)(2,1)S(1)} %collective-permute-done.42.refs_14_), channel_id=1, source_target_pairs={{0,1},{1,0},{2,3},{3,2},{4,5},{5,4},{6,7},{7,6},{8,9},{9,8},{10,11... | collective-permute-start | bytes 995336 | tf_op jit(solution)/shard_map/ppermute | solution.py:231
  253.1 14.2 %collective-permute-start.44 = (bf16[48,3456]{1,0:T(8,128)(2,1)S(1)}, bf16[48,3456]{1,0:T(8,128)(2,1)S(1)}, u32[]{:S(2)}, u32[]{:S(2)}) collective-permute-start(bf16[48,3456]{1,0:T(8,128)(2,1)S(1)} %collective-permute-done.42.refs_14_), channel_id=1, source_target_pairs={{0,2},{1,3},{2,0},{3,1},{4,6},{5,7},{6,4},{7,5},{8,10},{9,11},{10,... | collective-permute-start | bytes 995336 | tf_op jit(solution)/shard_map/ppermute | solution.py:231
  777.8 31.0 %collective-permute-start.62 = (bf16[16,48,1664]{2,1,0:T(8,128)(2,1)}, bf16[16,48,1664]{2,1,0:T(8,128)(2,1)}, u32[]{:S(2)}, u32[]{:S(2)}) collective-permute-start(bf16[16,48,1664]{2,1,0:T(8,128)(2,1)} %fusion.41), channel_id=1, source_target_pairs={{0,16},{16,0},{1,17},{17,1},{2,18},{18,2},{3,19},{19,3},{4,20},{20... | collective-permute-start | bytes 7667720 | tf_op jit(solution)/shard_map/ppermute | solution.py:235
  791.2 80.9 %collective-permute-start.79 = (bf16[16,48,3456]{2,1,0:T(8,128)(2,1)}, bf16[16,48,3456]{2,1,0:T(8,128)(2,1)}, u32[]{:S(2)}, u32[]{:S(2)}) collective-permute-start(bf16[16,48,3456]{2,1,0:T(8,128)(2,1)} %pad_maximum_fusion), channel_id=1, source_target_pairs={{0,16},{16,0},{1,17},{17,1},{2,18},{18,2},{3,19},{19,3},{4,20},{20... | collective-permute-start | bytes 15925256 | tf_op jit(solution)/shard_map/ppermute | solution.py:235
  835.6 16.9 %collective-permute-start.72 = (bf16[48,1664]{1,0:T(8,128)(2,1)}, bf16[48,1664]{1,0:T(8,128)(2,1)}, u32[]{:S(2)}, u32[]{:S(2)}) collective-permute-start(bf16[48,1664]{1,0:T(8,128)(2,1)} %get-tuple-element.126), channel_id=1, source_target_pairs={{0,2},{1,3},{2,0},{3,1},{4,6},{5,7},{6,4},{7,5},{8,10},{9,11},{10,... | collective-permute-start | bytes 479240 | tf_op jit(solution)/shard_map/ppermute | solution.py:231
  836.8 15.7 %collective-permute-start.75 = (bf16[48,1664]{1,0:T(8,128)(2,1)}, bf16[48,1664]{1,0:T(8,128)(2,1)}, u32[]{:S(2)}, u32[]{:S(2)}) collective-permute-start(bf16[48,1664]{1,0:T(8,128)(2,1)} %get-tuple-element.132), channel_id=1, source_target_pairs={{0,12},{1,13},{2,14},{3,15},{4,0},{5,1},{6,2},{7,3},{8,4},{9,5},{1... | collective-permute-start | bytes 479240 | tf_op jit(solution)/shard_map/ppermute | solution.py:231
  879.2 14.5 %collective-permute-start.90 = (bf16[48,3456]{1,0:T(8,128)(2,1)S(1)}, bf16[48,3456]{1,0:T(8,128)(2,1)S(1)}, u32[]{:S(2)}, u32[]{:S(2)}) collective-permute-start(bf16[48,3456]{1,0:T(8,128)(2,1)S(1)} %get-tuple-element.104), channel_id=1, source_target_pairs={{0,1},{1,0},{2,3},{3,2},{4,5},{5,4},{6,7},{7,6},{8,9},{9,8},{10,11... | collective-permute-start | bytes 995336 | tf_op jit(solution)/shard_map/ppermute | solution.py:231
  906.8 16.2 %collective-permute-start.83 = (bf16[48,3456]{1,0:T(8,128)(2,1)S(1)}, bf16[48,3456]{1,0:T(8,128)(2,1)S(1)}, u32[]{:S(2)}, u32[]{:S(2)}) collective-permute-start(bf16[48,3456]{1,0:T(8,128)(2,1)S(1)} %get-tuple-element.108), channel_id=1, source_target_pairs={{0,1},{1,0},{2,3},{3,2},{4,5},{5,4},{6,7},{7,6},{8,9},{9,8},{10,11... | collective-permute-start | bytes 995336 | tf_op jit(solution)/shard_map/ppermute | solution.py:231
  920.4 14.3 %collective-permute-start.80 = (bf16[48,3456]{1,0:T(8,128)(2,1)S(1)}, bf16[48,3456]{1,0:T(8,128)(2,1)S(1)}, u32[]{:S(2)}, u32[]{:S(2)}) collective-permute-start(bf16[48,3456]{1,0:T(8,128)(2,1)S(1)} %get-tuple-element.102), channel_id=1, source_target_pairs={{0,1},{1,0},{2,3},{3,2},{4,5},{5,4},{6,7},{7,6},{8,9},{9,8},{10,11... | collective-permute-start | bytes 995336 | tf_op jit(solution)/shard_map/ppermute | solution.py:231
  (243 other events, 2960.0 us)

commit v2 on v1

--- a/solution.py
+++ b/solution.py
@@ -243,18 +243,28 @@
     return [held[offset] for offset in OFFSETS]
 
 
-def scatter_units(units, origins):
-    sums = {
+def hold_back(later, sooner):
+    return lax.optimization_barrier((later, sooner))
+
+
+def scatter_start(units, origins):
+    return {
         offset: lax.dynamic_index_in_dim(units, origins[place], 0, keepdims=False).astype(F32)
         for place, offset in enumerate(OFFSETS)
     }
-    for round_steps in reversed(ROUNDS):
-        arrived = [
-            (offset, pass_on(sums[added(offset, step)].astype(BF), step, -1)) for offset, step in round_steps
-        ]
-        for offset, values in arrived:
-            sums[offset] = sums[offset] + values.astype(F32)
-    return sums[OFFSETS[0]]
+
+
+def scatter_send(sums, number):
+    return [
+        (offset, pass_on(sums[added(offset, step)].astype(BF), step, -1)) for offset, step in ROUNDS[4 - number]
+    ]
+
+
+def scatter_add(sums, arrived):
+    sums = dict(sums)
+    for offset, values in arrived:
+        sums[offset] = sums[offset] + values.astype(F32)
+    return sums
 
 
 def sum_small(values):
@@ -299,9 +309,10 @@
     return pl.pallas_call(
         functools.partial(place_kernel, plan, count),
         in_specs=[scalar, scalar] + [anywhere] * (2 * CHIPS),
-        out_specs=[anywhere] * len(shapes),
+        out_specs=[pl.BlockSpec(memory_space=pltpu.VMEM)] * len(shapes),
         out_shape=[jax.ShapeDtypeStruct(shape, BF) for shape in shapes],
         scratch_shapes=[pltpu.SemaphoreType.DMA((count,))],
+        compiler_params=pltpu.CompilerParams(vmem_limit_bytes=32 * 2**20),
     )(order, core, *own, *other)
 
 
@@ -387,10 +398,21 @@
     )
 
 
-def reduce_packed(pack, chip, core):
+def reduce_packed(pack, chip, core, waiting=()):
     arrived = swap_core(pack(1 - core).astype(BF))
     units = (pack(core).astype(F32) + arrived.astype(F32)).astype(BF)
-    mine = scatter_units(units, jnp.asarray(ORIGIN)[chip]).astype(BF)
+    sums = scatter_start(units, jnp.asarray(ORIGIN)[chip])
+    came = None
+    for number in range(5):
+        sent = scatter_send(sums, number)
+        if number < len(waiting):
+            waiting[number](came)
+        came = [values for _, values in sent]
+        sums = scatter_add(sums, sent)
+    for rest in waiting[5:]:
+        rest(came)
+        came = None
+    mine = sums[OFFSETS[0]].astype(BF)
     other = swap_core(mine)
     first = jnp.where(core == 0, mine, other).astype(F32)
     second = jnp.where(core == 0, other, mine).astype(F32)
@@ -417,10 +439,12 @@
     )
 
 
-def reduce_second(out, up, down, chip, core):
+def reduce_second(out, up, down, chip, core, waiting):
     if lax.axis_size("fsdp") != CHIPS:
+        for rest in waiting:
+            rest(None)
         return (reduce_plain(out, 0), reduce_plain(up, 0), reduce_plain(down, 0))
-    first, second = reduce_packed(lambda side: pack_second(out, up, down, side), chip, core)
+    first, second = reduce_packed(lambda side: pack_second(out, up, down, side), chip, core, waiting)
     return (
         jnp.concatenate([first[:, :384], second[:, :384]], axis=1),
         jnp.concatenate([first[:, 384:1920], second[:, 384:1920]], axis=1),
@@ -503,7 +527,7 @@
     return (first_new, second_new, direction)
 
 
-GROUPS = 3
+GROUPS = 6
 
 
 def on_device(
@@ -519,6 +543,7 @@
     weight_squares = jnp.stack([jnp.sum(matrix * matrix) for matrix in matrices])
     low = [matrix.astype(BF) for matrix in matrices]
     qkv_low, mod_turned, vector_low = gather_first(low[0], low[4], vectors.astype(BF), chip, core)
+    low[1:4], (qkv_low, mod_turned, vector_low) = hold_back(low[1:4], (qkv_low, mod_turned, vector_low))
     out_low, up_low, down_low = gather_second(low[1], low[2], low[3], chip, core)
 
     vector_all = vector_low.astype(F32)
@@ -569,13 +594,20 @@
     grad_branch = flat(grad_middle * gate_one).astype(BF)
     grad_attn_out = linear(attended_low, grad_branch, TN).astype(BF)
     grad_attended = linear(grad_branch, out_low, NT).astype(BF)
-    later = reduce_second(grad_attn_out, grad_up_weight, grad_down, chip, core)
-
     backward = []
-    for number, (part, query, key, value, feature) in enumerate(forward):
+
+    def backward_part(number, came):
+        part, query, key, value, feature = forward[number]
         width = per_call * PAIR
         grad_part = grad_attended[:, number * width : (number + 1) * width]
+        if came is not None:
+            grad_part, _ = hold_back(grad_part, came)
         backward.append(attention_backward(query, key, value, feature, feature_key, grad_part, part, cos, sin, per_call))
+
+    later = reduce_second(
+        grad_attn_out, grad_up_weight, grad_down, chip, core,
+        [functools.partial(backward_part, number) for number in range(GROUPS)],
+    )
     grad_mixed = jnp.concatenate([part[kind] for kind in range(3) for part in backward], axis=1)
     grad_qkv = linear(first_low, grad_mixed, TN).astype(BF)
     grad_first = tiled(linear(grad_mixed, qkv_low, NT))

time: 987 us -> 560 us (0.57)
  Pallas kernels: 550 us -> 86.3 us
  local copies, waits for them, and re-layouts: 60.5 us -> 98.1 us
  other arithmetic: 64.4 us -> 78.6 us
    pallas_call x2, Pallas kernels: 473 us -> 9.37 us  [place_units(): pl.pallas_call(functools.partial(place_kernel, plan, count), in_specs=[sc...]
    unnamed x359 -> x479, local copies, waits for them, and re-layouts: 29.7 us -> 72.1 us
    pallas_call x3 -> x6, Pallas kernels: 45.6 us -> 42.5 us  [attention_backward(): pl.pallas_call(functools.partial(attention_backward_kernel, block), grid=...]
    pallas_call x3 -> x6, Pallas kernels: 31.4 us -> 34.5 us  [attention_forward(): pl.pallas_call(functools.partial(attention_forward_kernel, block), grid=(...]
  transfers between devices with their start and end apart: 100 -> 100, of which waited for: 25 -> 27; matrix products, arithmetic and copies ran while one was open for 7% -> 12% of each run, Pallas kernels for 18% -> 13%
where the time goes in v2:
time: 560 us; the launch traced here: 551 us
  local copies, waits for them, and re-layouts  98.1 us (18%)
  matrix products  98.1 us (18%)
  Pallas kernels  86.3 us (15%)
  starting transfers between devices  81 us (14%)
  other arithmetic  78.6 us (14%)
  waiting for transfers between devices  71.8 us (13%)
  between operations  36.9 us (7%)
    dot_general x13, matrix products, linear(): lax.dot_general(left_side, right_side, dims, preferred_element_type=F32)  95.5 us
    ppermute x63, starting transfers between devices, pass_on(): lax.ppermute(values, 'fsdp', [(chip, moved(chip, step, sign)) for chip in...  73 us
    unnamed x479, local copies, waits for them, and re-layouts  72.1 us
    ppermute x63, waiting for transfers between devices, pass_on(): lax.ppermute(values, 'fsdp', [(chip, moved(chip, step, sign)) for chip in...  70.1 us
    pallas_call x6, Pallas kernels, attention_backward(): pl.pallas_call(functools.partial(attention_backward_kernel, block), grid=...  42.5 us
    pallas_call x6, Pallas kernels, attention_forward(): pl.pallas_call(functools.partial(attention_forward_kernel, block), grid=(...  34.5 us
  transfers between devices with their start and end apart: 100, of which 27 were waited for; matrix products, arithmetic and copies ran while one was open for 12% of the time, Pallas kernels for 13%

profile of v2, /device:TPU:0, one launch (start us, length us, event | category | flops | bytes accessed | tf_op | source)
XLA Modules:
  0.0 550.9 jit_solution(13863885251595576934)
XLA Ops:
  30.9 5.7 %collective-permute-done.6.refs_9_ = bf16[48,1664]{1,0:T(8,128)(2,1)S(1)} collective-permute-done((bf16[48,1664]{1,0:T(8,128)(2,1)S(1)}, bf16[48,1664]{1,0:T(8,128)(2,1)S(1)}, u32[]{:S(2)}, u32[]{:S(2)}) %collective-permute-start.6) | collective-permute-done | bytes 159776 | tf_op jit(solution)/shard_map/ppermute | solution.py:231
  93.8 8.0 %collective-permute-done.34.refs_6_ = bf16[48,3456]{1,0:T(8,128)(2,1)S(1)} collective-permute-done((bf16[48,3456]{1,0:T(8,128)(2,1)S(1)}, bf16[48,3456]{1,0:T(8,128)(2,1)S(1)}, u32[]{:S(2)}, u32[]{:S(2)}) %collective-permute-start.34) | collective-permute-done | bytes 331808 | tf_op jit(solution)/shard_map/ppermute | solution.py:231
  114.1 6.3 %fusion.142.q_ref.k_ref.v_ref = f32[1024,2304]{1,0:T(8,128)} fusion(bf16[1024,768]{1,0:T(8,128)(2,1)S(1)} %fusion.29, bf16[768,2304]{1,0:T(8,128)(2,1)S(1)} %copy-done.78), kind=kOutput, calls=%fused_computation.361 | convolution fusion | flops 3623878656 | bytes 14548992 | tf_op jit(solution)/shard_map/dot_general | solution.py:462
  120.4 5.7 %shard_map.404 = (bf16[1024,128]{1,0:T(8,128)(2,1)S(1)}, bf16[1024,128]{1,0:T(8,128)(2,1)S(1)}, bf16[1024,128]{1,0:T(8,128)(2,1)S(1)}, bf16[1024,128]{1,0:T(8,128)(2,1)S(1)}, bf16[1024,128]{1,0:T(8,128)(2,1)S(1)}) custom-call(f32[1024,2304]{1,0:T(8,128)} %fusion.142.q_ref.k_ref.v_ref, f32[1024,2304]{1,0:T(8,128)} %fusion.142.q_ref.k_ref.v_ref, ...), custom_call_target="tpu_custom_call" | custom-call | flops 2097152000 | bytes 3145728 | tf_op jit(solution)/shard_map/pallas_call | solution.py:103
  132.2 5.6 %shard_map.402 = (bf16[1024,128]{1,0:T(8,128)(2,1)S(1)}, bf16[1024,128]{1,0:T(8,128)(2,1)S(1)}, bf16[1024,128]{1,0:T(8,128)(2,1)S(1)}, bf16[1024,128]{1,0:T(8,128)(2,1)S(1)}, bf16[1024,128]{1,0:T(8,128)(2,1)S(1)}) custom-call(f32[1024,2304]{1,0:T(8,128)} %fusion.142.q_ref.k_ref.v_ref, f32[1024,2304]{1,0:T(8,128)} %fusion.142.q_ref.k_ref.v_ref, ...), custom_call_target="tpu_custom_call" | custom-call | flops 2097152000 | bytes 3145728 | tf_op jit(solution)/shard_map/pallas_call | solution.py:103
  137.9 6.1 %shard_map.401 = (bf16[1024,128]{1,0:T(8,128)(2,1)S(1)}, bf16[1024,128]{1,0:T(8,128)(2,1)S(1)}, bf16[1024,128]{1,0:T(8,128)(2,1)S(1)}, bf16[1024,128]{1,0:T(8,128)(2,1)S(1)}, bf16[1024,128]{1,0:T(8,128)(2,1)S(1)}) custom-call(f32[1024,2304]{1,0:T(8,128)} %fusion.142.q_ref.k_ref.v_ref, f32[1024,2304]{1,0:T(8,128)} %fusion.142.q_ref.k_ref.v_ref, ...), custom_call_target="tpu_custom_call" | custom-call | flops 2097152000 | bytes 3145728 | tf_op jit(solution)/shard_map/pallas_call | solution.py:103
  148.3 5.7 %shard_map.403 = (bf16[1024,128]{1,0:T(8,128)(2,1)S(1)}, bf16[1024,128]{1,0:T(8,128)(2,1)S(1)}, bf16[1024,128]{1,0:T(8,128)(2,1)S(1)}, bf16[1024,128]{1,0:T(8,128)(2,1)S(1)}, bf16[1024,128]{1,0:T(8,128)(2,1)S(1)}) custom-call(f32[1024,2304]{1,0:T(8,128)} %fusion.142.q_ref.k_ref.v_ref, f32[1024,2304]{1,0:T(8,128)} %fusion.142.q_ref.k_ref.v_ref, ...), custom_call_target="tpu_custom_call" | custom-call | flops 2097152000 | bytes 3145728 | tf_op jit(solution)/shard_map/pallas_call | solution.py:103
  161.0 5.8 %shard_map.405 = (bf16[1024,128]{1,0:T(8,128)(2,1)S(1)}, bf16[1024,128]{1,0:T(8,128)(2,1)S(1)}, bf16[1024,128]{1,0:T(8,128)(2,1)S(1)}, bf16[1024,128]{1,0:T(8,128)(2,1)S(1)}, bf16[1024,128]{1,0:T(8,128)(2,1)S(1)}) custom-call(f32[1024,2304]{1,0:T(8,128)} %fusion.142.q_ref.k_ref.v_ref, f32[1024,2304]{1,0:T(8,128)} %fusion.142.q_ref.k_ref.v_ref, ...), custom_call_target="tpu_custom_call" | custom-call | flops 2097152000 | bytes 3145728 | tf_op jit(solution)/shard_map/pallas_call | solution.py:103
  174.9 5.6 %shard_map.406 = (bf16[1024,128]{1,0:T(8,128)(2,1)S(1)}, bf16[1024,128]{1,0:T(8,128)(2,1)S(1)}, bf16[1024,128]{1,0:T(8,128)(2,1)S(1)}, bf16[1024,128]{1,0:T(8,128)(2,1)S(1)}, bf16[1024,128]{1,0:T(8,128)(2,1)S(1)}) custom-call(f32[1024,2304]{1,0:T(8,128)} %fusion.142.q_ref.k_ref.v_ref, f32[1024,2304]{1,0:T(8,128)} %fusion.142.q_ref.k_ref.v_ref, ...), custom_call_target="tpu_custom_call" | custom-call | flops 2097152000 | bytes 3145728 | tf_op jit(solution)/shard_map/pallas_call | solution.py:103
  216.5 8.0 %fusion.143 = f32[1024,3072]{1,0:T(8,128)} fusion(bf16[1024,768]{1,0:T(8,128)(2,1)S(1)} %fusion.28, bf16[768,3072]{1,0:T(8,128)(2,1)S(1)} %get-tuple-element.84), kind=kOutput, calls=%fused_computation.362 | convolution fusion | flops 4831838208 | bytes 18874368 | tf_op jit(solution)/shard_map/dot_general | solution.py:462
  224.5 12.5 %convolution_convert_fusion.1 = bf16[3072,768]{1,0:T(8,128)(2,1)} fusion(bf16[1024,768]{1,0:T(8,128)(2,1)S(1)} %copy-done.163, f32[1024,3072]{1,0:T(8,128)} %fusion.143, f32[3072]{0:T(1024)S(1)} %slice.330), kind=kOutput, calls=%fused_computation.27 | convolution fusion | flops 4865654784 | bytes 18886656 | tf_op jit(solution)/shard_map/dot_general | solution.py:462
  237.0 15.7 %fusion.140 = (bf16[3072]{0:T(1024)(128)(2,1)}, bf16[1024,3072]{1,0:T(8,128)(2,1)}) fusion(f32[1024,3072]{1,0:T(8,128)} %fusion.143, f32[3072]{0:T(1024)S(1)} %slice.330, bf16[1024,768]{1,0:T(8,128)(2,1)S(1)} %copy-done.163, bf16[3072,768]{1,0:T(8,128)(2,1)S(1)} %get-tuple-element.85), kind=kOutput, calls=%fused_computation.359 | convolution fusion | flops 4894749696 | bytes 25184256 | tf_op jit(solution)/shard_map/dot_general | solution.py:462
  252.7 9.7 %convolution_convert_fusion.2 = bf16[768,3072]{1,0:T(8,128)(2,1)} fusion(bf16[1024,768]{1,0:T(8,128)(2,1)S(1)} %fusion.28, bf16[1024,3072]{1,0:T(8,128)(2,1)} %get-tuple-element.267), kind=kOutput, calls=%fused_computation.28 | convolution fusion | flops 4834197504 | bytes 12582912 | tf_op jit(solution)/shard_map/dot_general | solution.py:462
  262.4 9.3 %fusion.39 = (f32[1024]{0:T(1024)S(1)}, f32[1024]{0:T(1024)S(1)}, f32[1024,768]{1,0:T(8,128)}) fusion(f32[8,768]{1,0:T(8,128)S(1)} %get-tuple-element.208, f32[1024]{0:T(1024)S(1)} %get-tuple-element.230, f32[1024]{0:T(1024)S(1)} %get-tuple-element.234, f32[1024,768]{1,0:T(8,128)S(1)} %copy-done.132, bf16[1,1024,768]{2,1,0:T(8,128)(2,1)S(1)} %copy-done.129, ...), kind=kOutput, calls=%fused_computation.81 | convolution fusion | flops 4838127616 | bytes 18915328 | tf_op jit(solution)/shard_map/dot_general | solution.py:462
  272.9 14.4 %fusion.17 = (bf16[1024,768]{1,0:T(8,128)(2,1)S(1)}, bf16[1024,768]{1,0:T(8,128)(2,1)}, f32[1024,768]{1,0:T(8,128)}) fusion(bf16[1,1024,768]{2,1,0:T(8,128)(2,1)S(1)} %copy-done.135, f32[1024,768]{1,0:T(8,128)} %get-tuple-element.263, f32[1024]{0:T(1024)S(1)} %get-tuple-element.236, f32[1024]{0:T(1024)S(1)} %get-tuple-element.232, ...), kind=kOutput, calls=%fused_computation.34 | convolution fusion | flops 4877451264 | bytes 33139712 | tf_op jit(solution)/shard_map/dot_general | solution.py:462
  341.8 7.1 %shard_map.408 = bf16[3,1024,128]{2,1,0:T(8,128)(2,1)S(1)} custom-call(bf16[1024,128]{1,0:T(8,128)(2,1)S(1)} %copy-done.121, bf16[1024,128]{1,0:T(8,128)(2,1)S(1)} %copy-done.123, bf16[1024,128]{1,0:T(8,128)(2,1)S(1)} %copy-done.125, bf16[1024,128]{1,0:T(8,128)(2,1)S(1)} %copy-done.127, bf16[1024,128]{1,0:T(8,128)(2,1)S(1)} %select_convert_fusion.fk_ref, ...), custom_call_target="tpu_custom_call" | custom-call | flops 4194304000 | bytes 2097152 | tf_op jit(solution)/shard_map/pallas_call | solution.py:178
  361.5 7.1 %shard_map.409 = bf16[3,1024,128]{2,1,0:T(8,128)(2,1)S(1)} custom-call(bf16[1024,128]{1,0:T(8,128)(2,1)S(1)} %copy-done.105, bf16[1024,128]{1,0:T(8,128)(2,1)S(1)} %copy-done.107, bf16[1024,128]{1,0:T(8,128)(2,1)S(1)} %copy-done.109, bf16[1024,128]{1,0:T(8,128)(2,1)S(1)} %copy-done.111, bf16[1024,128]{1,0:T(8,128)(2,1)S(1)} %select_convert_fusion.fk_ref, ...), custom_call_target="tpu_custom_call" | custom-call | flops 4194304000 | bytes 2097152 | tf_op jit(solution)/shard_map/pallas_call | solution.py:178
  374.3 7.1 %shard_map.410 = bf16[3,1024,128]{2,1,0:T(8,128)(2,1)S(1)} custom-call(bf16[1024,128]{1,0:T(8,128)(2,1)S(1)} %copy-done.113, bf16[1024,128]{1,0:T(8,128)(2,1)S(1)} %copy-done.115, bf16[1024,128]{1,0:T(8,128)(2,1)S(1)} %copy-done.117, bf16[1024,128]{1,0:T(8,128)(2,1)S(1)} %copy-done.119, bf16[1024,128]{1,0:T(8,128)(2,1)S(1)} %select_convert_fusion.fk_ref, ...), custom_call_target="tpu_custom_call" | custom-call | flops 4194304000 | bytes 2097152 | tf_op jit(solution)/shard_map/pallas_call | solution.py:178
  382.1 5.4 collective-permute-done.69
  391.4 7.1 %shard_map.411 = bf16[3,1024,128]{2,1,0:T(8,128)(2,1)S(1)} custom-call(bf16[1024,128]{1,0:T(8,128)(2,1)S(1)} %copy-done.81, bf16[1024,128]{1,0:T(8,128)(2,1)S(1)} %copy-done.83, bf16[1024,128]{1,0:T(8,128)(2,1)S(1)} %copy-done.85, bf16[1024,128]{1,0:T(8,128)(2,1)S(1)} %copy-done.87, bf16[1024,128]{1,0:T(8,128)(2,1)S(1)} %select_convert_fusion.fk_ref, ...), custom_call_target="tpu_custom_call" | custom-call | flops 4194304000 | bytes 2097152 | tf_op jit(solution)/shard_map/pallas_call | solution.py:178
  404.5 7.1 %shard_map.412 = bf16[3,1024,128]{2,1,0:T(8,128)(2,1)S(1)} custom-call(bf16[1024,128]{1,0:T(8,128)(2,1)S(1)} %copy-done.89, bf16[1024,128]{1,0:T(8,128)(2,1)S(1)} %copy-done.91, bf16[1024,128]{1,0:T(8,128)(2,1)S(1)} %copy-done.93, bf16[1024,128]{1,0:T(8,128)(2,1)S(1)} %copy-done.95, bf16[1024,128]{1,0:T(8,128)(2,1)S(1)} %select_convert_fusion.fk_ref, ...), custom_call_target="tpu_custom_call" | custom-call | flops 4194304000 | bytes 2097152 | tf_op jit(solution)/shard_map/pallas_call | solution.py:178
  412.5 7.1 %shard_map.413 = bf16[3,1024,128]{2,1,0:T(8,128)(2,1)S(1)} custom-call(bf16[1024,128]{1,0:T(8,128)(2,1)S(1)} %copy-done.97, bf16[1024,128]{1,0:T(8,128)(2,1)S(1)} %copy-done.99, bf16[1024,128]{1,0:T(8,128)(2,1)S(1)} %copy-done.101, bf16[1024,128]{1,0:T(8,128)(2,1)S(1)} %copy-done.103, bf16[1024,128]{1,0:T(8,128)(2,1)S(1)} %select_convert_fusion.fk_ref, ...), custom_call_target="tpu_custom_call" | custom-call | flops 4194304000 | bytes 2097152 | tf_op jit(solution)/shard_map/pallas_call | solution.py:178
  429.5 7.8 %convolution_convert_fusion.3 = bf16[768,2304]{1,0:T(8,128)(2,1)} fusion(bf16[1024,768]{1,0:T(8,128)(2,1)S(1)} %copy-done.162, bf16[1024,2304]{1,0:T(8,128)(2,1)} %fusion.78), kind=kOutput, calls=%fused_computation.29 | convolution fusion | flops 3625648128 | bytes 9830400 | tf_op jit(solution)/shard_map/dot_general | solution.py:462
  465.0 7.0 %fusion.25 = f32[1,1024,768]{2,1,0:T(8,128)} fusion(bf16[1,1024,768]{2,1,0:T(8,128)(2,1)S(1)} %copy-done.130, bf16[1,1024,768]{2,1,0:T(8,128)(2,1)S(1)} %copy-done.137, f32[1024,768]{1,0:T(8,128)} %copy-done.141, f32[1024,768]{1,0:T(8,128)} %get-tuple-element.263, f32[1024,768]{1,0:T(8,128)} %copy-done.131, f32[1024]{0:T(1024)S(1)} %broadcast_multiply_fusion, ...), kind=kLoop, calls=%fused_computation.48 | loop fusion | flops 15728640 | bytes 15814656 | tf_op jit(solution)/shard_map/add | solution.py:616
  (816 shorter events, 327.2 us)
Async XLA Ops:
  48.4 17.6 %collective-permute-start.26 = (bf16[48,1664]{1,0:T(8,128)(2,1)}, bf16[48,1664]{1,0:T(8,128)(2,1)}, u32[]{:S(2)}, u32[]{:S(2)}) collective-permute-start(bf16[48,1664]{1,0:T(8,128)(2,1)} %collective-permute-done.8.refs_13_), channel_id=1, source_target_pairs={{0,16},{16,0},{1,17},{17,1},{2,18},{18,2},{3,19},{19,3},{4,20},{20... | collective-permute-start | bytes 479240 | tf_op jit(solution)/shard_map/ppermute | solution.py:235
  48.7 17.4 %collective-permute-start.28 = (bf16[48,1664]{1,0:T(8,128)(2,1)}, bf16[48,1664]{1,0:T(8,128)(2,1)}, u32[]{:S(2)}, u32[]{:S(2)}) collective-permute-start(bf16[48,1664]{1,0:T(8,128)(2,1)} %collective-permute-done.12.refs_15_), channel_id=1, source_target_pairs={{0,16},{16,0},{1,17},{17,1},{2,18},{18,2},{3,19},{19,3},{4,20},{20... | collective-permute-start | bytes 479240 | tf_op jit(solution)/shard_map/ppermute | solution.py:235
  49.0 17.1 %collective-permute-start.29 = (bf16[48,1664]{1,0:T(8,128)(2,1)}, bf16[48,1664]{1,0:T(8,128)(2,1)}, u32[]{:S(2)}, u32[]{:S(2)}) collective-permute-start(bf16[48,1664]{1,0:T(8,128)(2,1)} %collective-permute-done.13.refs_16_), channel_id=1, source_target_pairs={{0,16},{16,0},{1,17},{17,1},{2,18},{18,2},{3,19},{19,3},{4,20},{20... | collective-permute-start | bytes 479240 | tf_op jit(solution)/shard_map/ppermute | solution.py:235
  89.8 17.2 %collective-permute-start.32 = (bf16[48,3456]{1,0:T(8,128)(2,1)S(1)}, bf16[48,3456]{1,0:T(8,128)(2,1)S(1)}, u32[]{:S(2)}, u32[]{:S(2)}) collective-permute-start(bf16[48,3456]{1,0:T(8,128)(2,1)S(1)} %maximum_bitcast_fusion.refs_2_), channel_id=1, source_target_pairs={{0,2},{1,3},{2,0},{3,1},{4,6},{5,7},{6,4},{7,5},{8,10},{9,11},{10,... | collective-permute-start | bytes 995336 | tf_op jit(solution)/shard_map/ppermute | solution.py:231
  90.7 17.9 %collective-permute-start.31 = (bf16[48,3456]{1,0:T(8,128)(2,1)S(1)}, bf16[48,3456]{1,0:T(8,128)(2,1)S(1)}, u32[]{:S(2)}, u32[]{:S(2)}) collective-permute-start(bf16[48,3456]{1,0:T(8,128)(2,1)S(1)} %maximum_bitcast_fusion.refs_2_), channel_id=1, source_target_pairs={{0,1},{1,0},{2,3},{3,2},{4,5},{5,4},{6,7},{7,6},{8,9},{9,8},{10,11... | collective-permute-start | bytes 995336 | tf_op jit(solution)/shard_map/ppermute | solution.py:231
  92.2 17.0 %collective-permute-start.46 = (bf16[48,3456]{1,0:T(8,128)(2,1)S(1)}, bf16[48,3456]{1,0:T(8,128)(2,1)S(1)}, u32[]{:S(2)}, u32[]{:S(2)}) collective-permute-start(bf16[48,3456]{1,0:T(8,128)(2,1)S(1)} %maximum_bitcast_fusion.refs_2_), channel_id=1, source_target_pairs={{0,16},{16,0},{1,17},{17,1},{2,18},{18,2},{3,19},{19,3},{4,20},{20... | collective-permute-start | bytes 995336 | tf_op jit(solution)/shard_map/ppermute | solution.py:235
  107.1 21.8 %collective-permute-start.35 = (bf16[48,3456]{1,0:T(8,128)(2,1)S(1)}, bf16[48,3456]{1,0:T(8,128)(2,1)S(1)}, u32[]{:S(2)}, u32[]{:S(2)}) collective-permute-start(bf16[48,3456]{1,0:T(8,128)(2,1)S(1)} %collective-permute-done.34.refs_6_), channel_id=1, source_target_pairs={{0,1},{1,0},{2,3},{3,2},{4,5},{5,4},{6,7},{7,6},{8,9},{9,8},{10,11... | collective-permute-start | bytes 995336 | tf_op jit(solution)/shard_map/ppermute | solution.py:231
  108.6 20.2 %collective-permute-start.33 = (bf16[48,3456]{1,0:T(8,128)(2,1)S(1)}, bf16[48,3456]{1,0:T(8,128)(2,1)S(1)}, u32[]{:S(2)}, u32[]{:S(2)}) collective-permute-start(bf16[48,3456]{1,0:T(8,128)(2,1)S(1)} %collective-permute-done.32.refs_4_), channel_id=1, source_target_pairs={{0,1},{1,0},{2,3},{3,2},{4,5},{5,4},{6,7},{7,6},{8,9},{9,8},{10,11... | collective-permute-start | bytes 995336 | tf_op jit(solution)/shard_map/ppermute | solution.py:231
  109.2 22.5 %collective-permute-start.48 = (bf16[48,3456]{1,0:T(8,128)(2,1)S(1)}, bf16[48,3456]{1,0:T(8,128)(2,1)S(1)}, u32[]{:S(2)}, u32[]{:S(2)}) collective-permute-start(bf16[48,3456]{1,0:T(8,128)(2,1)S(1)} %collective-permute-done.32.refs_4_), channel_id=1, source_target_pairs={{0,16},{16,0},{1,17},{17,1},{2,18},{18,2},{3,19},{19,3},{4,20},{20... | collective-permute-start | bytes 995336 | tf_op jit(solution)/shard_map/ppermute | solution.py:235
  111.2 20.4 %collective-permute-start.50 = (bf16[48,3456]{1,0:T(8,128)(2,1)S(1)}, bf16[48,3456]{1,0:T(8,128)(2,1)S(1)}, u32[]{:S(2)}, u32[]{:S(2)}) collective-permute-start(bf16[48,3456]{1,0:T(8,128)(2,1)S(1)} %collective-permute-done.34.refs_6_), channel_id=1, source_target_pairs={{0,16},{16,0},{1,17},{17,1},{2,18},{18,2},{3,19},{19,3},{4,20},{20... | collective-permute-start | bytes 995336 | tf_op jit(solution)/shard_map/ppermute | solution.py:235
  114.1 16.1 %collective-permute-start.47 = (bf16[48,3456]{1,0:T(8,128)(2,1)S(1)}, bf16[48,3456]{1,0:T(8,128)(2,1)S(1)}, u32[]{:S(2)}, u32[]{:S(2)}) collective-permute-start(bf16[48,3456]{1,0:T(8,128)(2,1)S(1)} %collective-permute-done.31.refs_3_), channel_id=1, source_target_pairs={{0,16},{16,0},{1,17},{17,1},{2,18},{18,2},{3,19},{19,3},{4,20},{20... | collective-permute-start | bytes 995336 | tf_op jit(solution)/shard_map/ppermute | solution.py:235
  128.9 17.5 %collective-permute-start.42 = (bf16[48,3456]{1,0:T(8,128)(2,1)S(1)}, bf16[48,3456]{1,0:T(8,128)(2,1)S(1)}, u32[]{:S(2)}, u32[]{:S(2)}) collective-permute-start(bf16[48,3456]{1,0:T(8,128)(2,1)S(1)} %collective-permute-done.38.refs_10_), channel_id=1, source_target_pairs={{0,4},{1,5},{2,6},{3,7},{4,8},{5,9},{6,10},{7,11},{8,12},{9,13},{1... | collective-permute-start | bytes 995336 | tf_op jit(solution)/shard_map/ppermute | solution.py:231
  128.9 17.9 %collective-permute-start.41 = (bf16[48,3456]{1,0:T(8,128)(2,1)S(1)}, bf16[48,3456]{1,0:T(8,128)(2,1)S(1)}, u32[]{:S(2)}, u32[]{:S(2)}) collective-permute-start(bf16[48,3456]{1,0:T(8,128)(2,1)S(1)} %collective-permute-done.38.refs_10_), channel_id=1, source_target_pairs={{0,2},{1,3},{2,0},{3,1},{4,6},{5,7},{6,4},{7,5},{8,10},{9,11},{10,... | collective-permute-start | bytes 995336 | tf_op jit(solution)/shard_map/ppermute | solution.py:231
  130.2 16.0 %collective-permute-start.37 = (bf16[48,3456]{1,0:T(8,128)(2,1)S(1)}, bf16[48,3456]{1,0:T(8,128)(2,1)S(1)}, u32[]{:S(2)}, u32[]{:S(2)}) collective-permute-start(bf16[48,3456]{1,0:T(8,128)(2,1)S(1)} %collective-permute-done.36.refs_8_), channel_id=1, source_target_pairs={{0,1},{1,0},{2,3},{3,2},{4,5},{5,4},{6,7},{7,6},{8,9},{9,8},{10,11... | collective-permute-start | bytes 995336 | tf_op jit(solution)/shard_map/ppermute | solution.py:231
  131.7 15.7 %collective-permute-start.49 = (bf16[48,3456]{1,0:T(8,128)(2,1)S(1)}, bf16[48,3456]{1,0:T(8,128)(2,1)S(1)}, u32[]{:S(2)}, u32[]{:S(2)}) collective-permute-start(bf16[48,3456]{1,0:T(8,128)(2,1)S(1)} %collective-permute-done.33.refs_5_), channel_id=1, source_target_pairs={{0,16},{16,0},{1,17},{17,1},{2,18},{18,2},{3,19},{19,3},{4,20},{20... | collective-permute-start | bytes 995336 | tf_op jit(solution)/shard_map/ppermute | solution.py:235
  131.7 16.5 %collective-permute-start.51 = (bf16[48,3456]{1,0:T(8,128)(2,1)S(1)}, bf16[48,3456]{1,0:T(8,128)(2,1)S(1)}, u32[]{:S(2)}, u32[]{:S(2)}) collective-permute-start(bf16[48,3456]{1,0:T(8,128)(2,1)S(1)} %collective-permute-done.35.refs_7_), channel_id=1, source_target_pairs={{0,16},{16,0},{1,17},{17,1},{2,18},{18,2},{3,19},{19,3},{4,20},{20... | collective-permute-start | bytes 995336 | tf_op jit(solution)/shard_map/ppermute | solution.py:235
  169.8 15.3 %collective-permute-start.55 = (bf16[48,3456]{1,0:T(8,128)(2,1)S(1)}, bf16[48,3456]{1,0:T(8,128)(2,1)S(1)}, u32[]{:S(2)}, u32[]{:S(2)}) collective-permute-start(bf16[48,3456]{1,0:T(8,128)(2,1)S(1)} %collective-permute-done.40.refs_11_), channel_id=1, source_target_pairs={{0,16},{16,0},{1,17},{17,1},{2,18},{18,2},{3,19},{19,3},{4,20},{20... | collective-permute-start | bytes 995336 | tf_op jit(solution)/shard_map/ppermute | solution.py:235
  298.6 35.2 %collective-permute-start.62 = (bf16[16,48,3456]{2,1,0:T(8,128)(2,1)}, bf16[16,48,3456]{2,1,0:T(8,128)(2,1)}, u32[]{:S(2)}, u32[]{:S(2)}) collective-permute-start(bf16[16,48,3456]{2,1,0:T(8,128)(2,1)} %pad_maximum_fusion), channel_id=1, source_target_pairs={{0,16},{16,0},{1,17},{17,1},{2,18},{18,2},{3,19},{19,3},{4,20},{20... | collective-permute-start | bytes 15925256 | tf_op jit(solution)/shard_map/ppermute | solution.py:235
  351.2 18.2 %collective-permute-start.67 = (bf16[48,3456]{1,0:T(8,128)(2,1)S(1)}, bf16[48,3456]{1,0:T(8,128)(2,1)S(1)}, u32[]{:S(2)}, u32[]{:S(2)}) collective-permute-start(bf16[48,3456]{1,0:T(8,128)(2,1)S(1)} %get-tuple-element.159), channel_id=1, source_target_pairs={{0,2},{1,3},{2,0},{3,1},{4,6},{5,7},{6,4},{7,5},{8,10},{9,11},{10,... | collective-permute-start | bytes 995336 | tf_op jit(solution)/shard_map/ppermute | solution.py:231
  352.4 29.7 %collective-permute-start.70 = (bf16[48,3456]{1,0:T(8,128)(2,1)S(1)}, bf16[48,3456]{1,0:T(8,128)(2,1)S(1)}, u32[]{:S(2)}, u32[]{:S(2)}) collective-permute-start(bf16[48,3456]{1,0:T(8,128)(2,1)S(1)} %get-tuple-element.158), channel_id=1, source_target_pairs={{0,2},{1,3},{2,0},{3,1},{4,6},{5,7},{6,4},{7,5},{8,10},{9,11},{10,... | collective-permute-start | bytes 995336 | tf_op jit(solution)/shard_map/ppermute | solution.py:231
  353.2 19.6 %collective-permute-start.66 = (bf16[48,3456]{1,0:T(8,128)(2,1)S(1)}, bf16[48,3456]{1,0:T(8,128)(2,1)S(1)}, u32[]{:S(2)}, u32[]{:S(2)}) collective-permute-start(bf16[48,3456]{1,0:T(8,128)(2,1)S(1)} %get-tuple-element.160), channel_id=1, source_target_pairs={{0,1},{1,0},{2,3},{3,2},{4,5},{5,4},{6,7},{7,6},{8,9},{9,8},{10,11... | collective-permute-start | bytes 995336 | tf_op jit(solution)/shard_map/ppermute | solution.py:231
  353.8 45.5 %collective-permute-start.72 = (bf16[48,3456]{1,0:T(8,128)(2,1)S(1)}, bf16[48,3456]{1,0:T(8,128)(2,1)S(1)}, u32[]{:S(2)}, u32[]{:S(2)}) collective-permute-start(bf16[48,3456]{1,0:T(8,128)(2,1)S(1)} %get-tuple-element.157), channel_id=1, source_target_pairs={{0,1},{1,0},{2,3},{3,2},{4,5},{5,4},{6,7},{7,6},{8,9},{9,8},{10,11... | collective-permute-start | bytes 995336 | tf_op jit(solution)/shard_map/ppermute | solution.py:231
  369.4 43.0 %collective-permute-start.75 = (bf16[48,3456]{1,0:T(8,128)(2,1)S(1)}, bf16[48,3456]{1,0:T(8,128)(2,1)S(1)}, u32[]{:S(2)}, u32[]{:S(2)}) collective-permute-start(bf16[48,3456]{1,0:T(8,128)(2,1)S(1)} %get-tuple-element.156), channel_id=1, source_target_pairs={{0,1},{1,0},{2,3},{3,2},{4,5},{5,4},{6,7},{7,6},{8,9},{9,8},{10,11... | collective-permute-start | bytes 995336 | tf_op jit(solution)/shard_map/ppermute | solution.py:231
  372.2 15.3 %collective-permute-start.69 = (bf16[48,3456]{1,0:T(8,128)(2,1)S(1)}, bf16[48,3456]{1,0:T(8,128)(2,1)S(1)}, u32[]{:S(2)}, u32[]{:S(2)}) collective-permute-start(bf16[48,3456]{1,0:T(8,128)(2,1)S(1)} %get-tuple-element.167), channel_id=1, source_target_pairs={{0,1},{1,0},{2,3},{3,2},{4,5},{5,4},{6,7},{7,6},{8,9},{9,8},{10,11... | collective-permute-start | bytes 995336 | tf_op jit(solution)/shard_map/ppermute | solution.py:231
  (297 other events, 3000.4 us)
